TPU v7x, 256 devices: a whole 4x4x8 slice. The times are simulated.
256 devices in a mesh: batch: 8 (over z), proto: 32 (over x, y, core).
Axes of the slice: x: 4, y: 4, z: 8, core: 2. Of those that a mesh axis runs over, the one named last changes fastest.
Arguments:
- teacher_feat: bfloat16 [2048, 256], P('batch'), may hold values from -16 to 16
- student_feat: bfloat16 [8192, 256], P('batch'), may hold values from -16 to 16
- head_weight: bfloat16 [256, 131072], P(None, 'proto'), may hold values from -0.25 to 0.25
- pairing: int32 [8192], P('batch'), may hold values from 0 to 2047, as said below
Outputs:
- loss: float32 [], replicated
- d_student: float32 [8192, 256], P(('batch', 'proto'))
- d_weight: float32 [256, 131072], P('batch', 'proto')
Inputs may be any that keep to these rules, and one draw needn't show every extreme that they name: Student row j is paired with a teacher row of its own batch block: pairing[j] // 256 == j // 1024; each teacher row is named by exactly 4 student rows.
All inputs are finite; a program needn't handle non-finite values.
Results may differ from a plain program's by a relative error of at most 0.0045.
Values sent between devices are 32-bit elements; how exact they have to be, the bound alone decides.
No kernel may reach another device: no remote copies, remote signals or barrier semaphores. Data moves between devices by JAX's collectives and lax.ppermute only.
A program may use at most 128 MiB of HBM per device.

v0:
```python
import math

import jax
import jax.numpy as jnp
from jax import lax
from jax.experimental import pallas as pl
from jax.experimental.pallas import tpu as pltpu
from jax.sharding import PartitionSpec as P

ITERS = 3
LANES = 128
S_CHUNK = 512
T_CHUNK = 1024
TEACHER_TEMP = 0.07
STUDENT_TEMP = 0.1
LOG2E = math.log2(math.e)
T_SCALE = LOG2E / TEACHER_TEMP
S_SCALE = LOG2E / STUDENT_TEMP
F32 = jnp.float32
BF16 = jnp.bfloat16
NN = (((1,), (0,)), ((), ()))
NT = (((1,), (1,)), ((), ()))
TN = (((0,), (0,)), ((), ()))
VMEM_LIMIT = 60 * 1024 * 1024


def mm(a, b, dims):
    return lax.dot_general(a, b, dims, preferred_element_type=F32)


def halves(x):
    high = x.astype(BF16)
    return high, (x - high.astype(F32)).astype(BF16)


def by_sublane(x, combine):
    return combine(x.reshape(x.shape[0] // 8, 8, x.shape[1]), axis=0)


def whole(shape):
    return pl.BlockSpec(shape, lambda c: (0,) * len(shape))


def call(
    body, grid, in_specs, out_specs, out_shape, scratch, flops, transcendentals, size, aliases=None
):
    return pl.pallas_call(
        body,
        grid=(grid,),
        in_specs=in_specs,
        out_specs=out_specs,
        out_shape=out_shape,
        scratch_shapes=scratch,
        input_output_aliases=aliases or {},
        cost_estimate=pl.CostEstimate(
            flops=flops, transcendentals=transcendentals, bytes_accessed=size
        ),
        compiler_params=pltpu.CompilerParams(
            dimension_semantics=("arbitrary",), vmem_limit_bytes=VMEM_LIMIT
        ),
    )


def struct(shape, dtype=F32):
    return jax.ShapeDtypeStruct(shape, dtype)


def put_rows(ref, first, row):
    for i in range(row.shape[1] // LANES):
        ref[first + i : first + i + 1, :] = row[:, i * LANES : (i + 1) * LANES]


def turned(tf):
    def body(tf_ref, out_ref):
        out_ref[...] = tf_ref[...].astype(F32).T

    return call(
        body, 1, [whole(tf.shape)], [whole(tf.shape[::-1])], [struct(tf.shape[::-1])], [], 0, 0, 2**18
    )(tf)[0]


def student_stats(sf, tf, w, peers):
    rows, width = sf.shape
    t_rows = tf.shape[0]
    columns = w.shape[1]
    steps = columns // S_CHUNK
    s_rows, tr = rows // LANES, t_rows // LANES
    lines = -(-(2 * s_rows + tr) // 8) * 8

    def body(sf_ref, tf_ref, w_ref, wt_ref, out_ref, high, total, t_high, line):
        step = pl.program_id(0)

        @pl.when(step == 0)
        def _():
            high[...] = jnp.full_like(high, -3e38)
            total[...] = jnp.zeros_like(total)
            t_high[...] = jnp.full_like(t_high, -3e38)

        wt = w_ref[...].T
        wt_ref[...] = wt
        scores = mm(wt, sf_ref[...], NT)
        before = high[...]
        now = jnp.maximum(before, by_sublane(scores, jnp.max))
        high[...] = now
        groups = scores.reshape(S_CHUNK // 8, 8, rows)
        part = jnp.sum(jnp.exp2((groups - now[None]) * S_SCALE), axis=0)
        total[...] = total[...] * jnp.exp2((before - now) * S_SCALE) + part
        t_high[...] = jnp.maximum(t_high[...], by_sublane(mm(wt, tf_ref[...], NT), jnp.max))

        @pl.when(step == steps - 1)
        def _():
            best = jnp.max(high[...], axis=0, keepdims=True)
            summed = jnp.sum(
                total[...] * jnp.exp2((high[...] - best) * S_SCALE), axis=0, keepdims=True
            )
            line[...] = jnp.zeros_like(line)
            put_rows(line, 0, best)
            put_rows(line, s_rows, summed)
            put_rows(line, 2 * s_rows, jnp.max(t_high[...], axis=0, keepdims=True))
            out_ref[...] = jnp.broadcast_to(line[...][None], out_ref.shape)

    return call(
        body,
        steps,
        [
            whole(sf.shape),
            whole(tf.shape),
            pl.BlockSpec((width, S_CHUNK), lambda c: (0, c)),
        ],
        [
            pl.BlockSpec((S_CHUNK, width), lambda c: (c, 0)),
            whole((peers, lines, LANES)),
        ],
        [
            struct((columns, width), BF16),
            struct((peers, lines, LANES)),
        ],
        [
            pltpu.VMEM((8, rows), F32),
            pltpu.VMEM((8, rows), F32),
            pltpu.VMEM((8, t_rows), F32),
            pltpu.VMEM((lines, LANES), F32),
        ],
        2 * columns * width * (rows + t_rows),
        columns * rows,
        8 * 2**20,
    )(sf, tf, w)


def merge_stats(stats, gt, rows, batches):
    width, t_rows = gt.shape
    share = width // batches
    s_rows, tr = rows // LANES, t_rows // LANES

    def body(stats_ref, gt_ref, lse_ref, out_ref):
        highs = stats_ref[:, :s_rows, :]
        best = jnp.max(highs, axis=0)
        total = jnp.sum(
            stats_ref[:, s_rows : 2 * s_rows, :] * jnp.exp2((highs - best[None]) * S_SCALE), axis=0
        )
        lse_ref[...] = best * S_SCALE + jnp.log2(total)
        t_best = jnp.max(stats_ref[:, 2 * s_rows : 2 * s_rows + tr, :], axis=0) * T_SCALE
        row = jnp.concatenate([t_best[i : i + 1, :] for i in range(tr)], axis=1)
        for b in range(batches):
            out_ref[b, :share, :] = gt_ref[b * share : (b + 1) * share, :]
            out_ref[b, share:, :] = jnp.broadcast_to(row, (8, t_rows))

    return call(
        body,
        1,
        [whole(stats.shape), whole(gt.shape)],
        [whole((s_rows, LANES)), whole((batches, share + 8, t_rows))],
        [struct((s_rows, LANES)), struct((batches, share + 8, t_rows))],
        [],
        stats.size * 4,
        stats.size,
        2**21,
    )(stats, gt)


def student_grads(sf, w, wt, lse, half, before, peers):
    rows, width = sf.shape
    columns = w.shape[1]
    steps = columns // S_CHUNK // 2
    first = half * steps
    s_rows = rows // LANES

    def body(sf_ref, w_ref, wt_ref, lse_ref, *rest):
        if half:
            _, old_ref, ds_ref, dw_ref, lse_row, sft, acc = rest
        else:
            ds_ref, dw_ref, lse_row, sft, acc = rest
        step = pl.program_id(0)

        @pl.when(step == 0)
        def _():
            for i in range(s_rows):
                lse_row[:, i * LANES : (i + 1) * LANES] = lse_ref[i : i + 1, :]
            sft[...] = sf_ref[...].T
            acc[...] = old_ref[...] if half else jnp.zeros_like(acc)

        scores = mm(wt_ref[...], sf_ref[...], NT)
        high, low = halves(jnp.exp2(scores * S_SCALE - lse_row[...]))
        acc[...] += mm(w_ref[...], high, NN) + mm(w_ref[...], low, NN)
        dw_ref[...] = (mm(sft[...], high, NT) + mm(sft[...], low, NT)) / STUDENT_TEMP

        @pl.when(step == steps - 1)
        def _():
            if half:
                ds_ref[...] = (acc[...].T / STUDENT_TEMP).reshape(ds_ref.shape)
            else:
                ds_ref[...] = acc[...]

    ds_shape = (peers, rows // peers, width) if half else (width, rows)
    in_specs = [
        whole(sf.shape),
        pl.BlockSpec((width, S_CHUNK), lambda c: (0, c + first)),
        pl.BlockSpec((S_CHUNK, width), lambda c: (c + first, 0)),
        whole(lse.shape),
    ]
    operands = [sf, w, wt, lse]
    if half:
        in_specs += [pl.BlockSpec(memory_space=pl.ANY), whole((width, rows))]
        operands += [before[1], before[0]]
    return call(
        body,
        steps,
        in_specs,
        [whole(ds_shape), pl.BlockSpec((width, S_CHUNK), lambda c: (0, c + first))],
        [struct(ds_shape), struct((width, columns))],
        [
            pltpu.VMEM((1, rows), F32),
            pltpu.VMEM((width, rows), BF16),
            pltpu.VMEM((width, rows), F32),
        ],
        8 * columns * width * rows,
        columns * rows // 2,
        6 * 2**20,
        {4: 1} if half else None,
    )(*operands)


def fill_offsets(offset, packed, blocks, per_block):
    for i in range(blocks):
        for j in range(per_block):
            line = i * per_block + j
            offset[i : i + 1, j * LANES : (j + 1) * LANES] = packed[line : line + 1, :]


def expos_and_scale(wt, feats, offset, expo, blocks, all_columns):
    partial = None
    for i in range(blocks):
        scores = mm(wt, feats[i], NN)
        values = jnp.exp2(scores * T_SCALE - offset[i : i + 1, :])
        expo[i] = values
        for j in range(values.shape[1] // LANES):
            piece = values[:, j * LANES : (j + 1) * LANES]
            partial = piece if partial is None else partial + piece
    return 1.0 / (all_columns * jnp.sum(partial, axis=1, keepdims=True))


def add_rows(expo, scale, mass, blocks):
    for i in range(blocks):
        mass[i] += by_sublane(expo[i] * scale, jnp.sum)


def put_mass(mass, line, blocks):
    for i in range(blocks):
        row = jnp.sum(mass[i], axis=0, keepdims=True)
        put_rows(line, i * (row.shape[1] // LANES), row)


def first_iteration(feats_f32, shared, wt, passed, peers):
    blocks, width, t_rows = feats_f32.shape
    columns = wt.shape[0]
    steps = columns // T_CHUNK
    tr = t_rows // LANES
    share = shared.shape[1] - 8

    def body(
        feat_ref, shared_ref, wt_ref, _,
        feat_out, off_out, out_ref, __, offset, expo, mass, line,
    ):
        step = pl.program_id(0)

        @pl.when(step == 0)
        def _():
            feat_out[...] = feat_ref[...].astype(BF16)
            for i in range(blocks):
                row = shared_ref[i, share : share + 1, :]
                offset[i : i + 1, :] = row
                put_rows(off_out, i * tr, row)
            mass[...] = jnp.zeros_like(mass)

        scale = expos_and_scale(wt_ref[...], feat_out, offset, expo, blocks, columns * peers)
        add_rows(expo, scale, mass, blocks)

        @pl.when(step == steps - 1)
        def _():
            put_mass(mass, line, blocks)
            out_ref[...] = jnp.broadcast_to(line[...][None], out_ref.shape)

    return call(
        body,
        steps,
        [
            whole(feats_f32.shape),
            whole(shared.shape),
            pl.BlockSpec((T_CHUNK, width), lambda c: (c, 0)),
            pl.BlockSpec(memory_space=pl.ANY),
        ],
        [
            whole(feats_f32.shape),
            whole((blocks * tr, LANES)),
            whole((peers, blocks * tr, LANES)),
            pl.BlockSpec(memory_space=pl.ANY),
        ],
        [
            struct(feats_f32.shape, BF16),
            struct((blocks * tr, LANES)),
            struct((peers, blocks * tr, LANES)),
            struct(passed.shape),
        ],
        [
            pltpu.VMEM((max(blocks, 8), t_rows), F32),
            pltpu.VMEM((blocks, T_CHUNK, t_rows), F32),
            pltpu.VMEM((blocks, 8, t_rows), F32),
            pltpu.VMEM((blocks * tr, LANES), F32),
        ],
        5 * columns * width * t_rows * blocks,
        columns * t_rows * blocks,
        5 * 2**20,
        {3: 3},
    )(feats_f32, shared, wt, passed)


def next_iteration(feats, old, received, wt, passed):
    blocks, width, t_rows = feats.shape
    columns = wt.shape[0]
    peers = received.shape[0]
    steps = columns // T_CHUNK
    tr = t_rows // LANES
    total_t = blocks * t_rows

    def body(
        feat_ref, old_ref, recv_ref, wt_ref, _,
        off_out, out_ref, __, offset, expo, mass, line,
    ):
        step = pl.program_id(0)

        @pl.when(step == 0)
        def _():
            packed = old_ref[...] + jnp.log2(total_t * jnp.sum(recv_ref[...], axis=0))
            off_out[...] = packed
            fill_offsets(offset, packed, blocks, tr)
            mass[...] = jnp.zeros_like(mass)

        scale = expos_and_scale(wt_ref[...], feat_ref, offset, expo, blocks, columns * peers)
        add_rows(expo, scale, mass, blocks)

        @pl.when(step == steps - 1)
        def _():
            put_mass(mass, line, blocks)
            out_ref[...] = jnp.broadcast_to(line[...][None], out_ref.shape)

    return call(
        body,
        steps,
        [
            whole(feats.shape),
            whole(old.shape),
            whole(received.shape),
            pl.BlockSpec((T_CHUNK, width), lambda c: (c, 0)),
            pl.BlockSpec(memory_space=pl.ANY),
        ],
        [
            whole(old.shape),
            whole((peers, blocks * tr, LANES)),
            pl.BlockSpec(memory_space=pl.ANY),
        ],
        [struct(old.shape), struct((peers, blocks * tr, LANES)), struct(passed.shape)],
        [
            pltpu.VMEM((max(blocks, 8), t_rows), F32),
            pltpu.VMEM((blocks, T_CHUNK, t_rows), F32),
            pltpu.VMEM((blocks, 8, t_rows), F32),
            pltpu.VMEM((blocks * tr, LANES), F32),
        ],
        5 * columns * width * t_rows * blocks,
        columns * t_rows * blocks,
        4 * 2**20,
        {4: 2},
    )(feats, old, received, wt, passed)


def last_iteration(me, feats, old, received, w, wt, gt):
    blocks, width, t_rows = feats.shape
    columns = wt.shape[0]
    peers = received.shape[0]
    steps = columns // T_CHUNK
    tr = t_rows // LANES
    total_t = blocks * t_rows
    lines = -(-(blocks * tr + tr) // 8) * 8

    def body(
        me_ref, feat_ref, old_ref, recv_ref, w_ref, wt_ref, gt_ref,
        off_out, scale_out, taught_ref, out_ref, offset, expo, mass, line, acc, w_last, high, low,
    ):
        step = pl.program_id(0)

        @pl.when(step == 0)
        def _():
            packed = old_ref[...] + jnp.log2(total_t * jnp.sum(recv_ref[...], axis=0))
            off_out[...] = packed
            fill_offsets(offset, packed, blocks, tr)
            mass[...] = jnp.zeros_like(mass)
            acc[...] = jnp.zeros_like(acc)
            w_last[...] = jnp.zeros_like(w_last)
            high[...] = jnp.zeros_like(high)
            low[...] = jnp.zeros_like(low)

        def add_taught():
            acc[...] += mm(w_last[...], high[...], NN) + mm(w_last[...], low[...], NN)

        scale = expos_and_scale(wt_ref[...], feat_ref, offset, expo, blocks, columns * peers)
        scale_out[...] = jnp.broadcast_to(scale, scale_out.shape)
        add_taught()
        add_rows(expo, scale, mass, blocks)
        high[...], low[...] = halves(expo[me_ref[0]] * scale)
        w_last[...] = w_ref[...]

        @pl.when(step == steps - 1)
        def _():
            add_taught()
            line[...] = jnp.zeros_like(line)
            put_mass(mass, line, blocks)
            put_rows(line, blocks * tr, jnp.sum(acc[...] * gt_ref[...], axis=0, keepdims=True))
            out_ref[...] = jnp.broadcast_to(line[...][None], out_ref.shape)
            taught_ref[...] = acc[...]

    return call(
        body,
        steps,
        [
            pl.BlockSpec(memory_space=pltpu.SMEM),
            whole(feats.shape),
            whole(old.shape),
            whole(received.shape),
            pl.BlockSpec((width, T_CHUNK), lambda c: (0, c)),
            pl.BlockSpec((T_CHUNK, width), lambda c: (c, 0)),
            whole(gt.shape),
        ],
        [
            whole(old.shape),
            pl.BlockSpec((T_CHUNK, LANES), lambda c: (c, 0)),
            whole((width, t_rows)),
            whole((peers, lines, LANES)),
        ],
        [
            struct(old.shape),
            struct((columns, LANES)),
            struct((width, t_rows)),
            struct((peers, lines, LANES)),
        ],
        [
            pltpu.VMEM((max(blocks, 8), t_rows), F32),
            pltpu.VMEM((blocks, T_CHUNK, t_rows), F32),
            pltpu.VMEM((blocks, 8, t_rows), F32),
            pltpu.VMEM((lines, LANES), F32),
            pltpu.VMEM((width, t_rows), F32),
            pltpu.VMEM((width, T_CHUNK), BF16),
            pltpu.VMEM((T_CHUNK, t_rows), BF16),
            pltpu.VMEM((T_CHUNK, t_rows), BF16),
        ],
        2 * columns * width * t_rows * (blocks + 2),
        columns * t_rows * blocks,
        8 * 2**20,
    )(me, feats, old, received, w, wt, gt)


def after_iterations(me, received, lse, taught, onehot, ds_prob, blocks):
    width, t_rows = taught.shape
    tr = t_rows // LANES
    n = blocks * tr

    def body(me_ref, recv_ref, lse_ref, taught_ref, oh_ref, prob_ref, part_ref, inv_ref, ds_ref):
        total = jnp.sum(recv_ref[...], axis=0)
        inv_ref[...] = 1.0 / total[:n]
        start = me_ref[0] * tr
        inverse = 1.0 / jnp.sum(recv_ref[:, pl.ds(start, tr), :], axis=0)
        product = jnp.sum(total[n : n + tr] * inverse) / STUDENT_TEMP
        part_ref[...] = jnp.full(part_ref.shape, jnp.sum(lse_ref[...]) / LOG2E - product, F32)
        row = jnp.concatenate([inverse[i : i + 1, :] for i in range(tr)], axis=1)
        high, low = halves(taught_ref[...] * row / STUDENT_TEMP)
        wanted = mm(oh_ref[...], high, NT) + mm(oh_ref[...], low, NT)
        ds_ref[...] = prob_ref[...] - wanted.reshape(ds_ref.shape)

    return call(
        body,
        1,
        [
            pl.BlockSpec(memory_space=pltpu.SMEM),
            whole(received.shape),
            whole(lse.shape),
            whole(taught.shape),
            whole(onehot.shape),
            whole(ds_prob.shape),
        ],
        [whole((8, LANES)), whole((n, LANES)), whole(ds_prob.shape)],
        [struct((8, LANES)), struct((n, LANES)), struct(ds_prob.shape)],
        [],
        4 * onehot.size * width,
        1024,
        3 * 2**20,
    )(me, received, lse, taught, onehot, ds_prob)


def weight_grad(feats, offset_packed, inverse, wt, shared, scale, all_columns):
    blocks, width, t_rows = feats.shape
    columns = wt.shape[0]
    steps = columns // T_CHUNK
    tr = t_rows // LANES
    share = shared.shape[1] - 8

    def body(feat_ref, off_ref, inv_ref, wt_ref, sh_ref, scale_ref, out_ref, offset, g, g_sum):
        @pl.when(pl.program_id(0) == 0)
        def _():
            fill_offsets(offset, off_ref[...] - jnp.log2(inv_ref[...]), blocks, tr)
            total = jnp.zeros((8, LANES), F32)
            for i in range(blocks):
                high, low = halves(sh_ref[i, :share, :] / STUDENT_TEMP)
                part = jnp.concatenate([high, low, jnp.zeros((LANES - 2 * share, t_rows), BF16)])
                g[i] = part
                total += mm(jnp.ones((8, t_rows), BF16), part, NT)
            g_sum[...] = total

        middle = 1.0 / (all_columns * scale_ref[...])
        wide = jnp.concatenate([middle] * tr, axis=1)
        acc = middle * g_sum[0:1, :]
        for i in range(blocks):
            scores = mm(wt_ref[...], feat_ref[i], NN)
            expo = jnp.exp2(scores * T_SCALE - offset[i : i + 1, :])
            acc += mm((expo - wide).astype(BF16), g[i], NT)
        out = (acc * scale_ref[...]).T
        out_ref[...] = out[:share] + out[share : 2 * share]

    return call(
        body,
        steps,
        [
            whole(feats.shape),
            whole(offset_packed.shape),
            whole(inverse.shape),
            pl.BlockSpec((T_CHUNK, width), lambda c: (c, 0)),
            whole(shared.shape),
            pl.BlockSpec((T_CHUNK, LANES), lambda c: (c, 0)),
        ],
        [pl.BlockSpec((share, T_CHUNK), lambda c: (0, c))],
        [struct((share, columns))],
        [
            pltpu.VMEM((max(blocks, 8), t_rows), F32),
            pltpu.VMEM((blocks, LANES, t_rows), BF16),
            pltpu.VMEM((8, LANES), F32),
        ],
        6 * columns * width * t_rows * blocks,
        columns * t_rows * blocks,
        6 * 2**20,
    )(feats, offset_packed, inverse, wt, shared, scale)[0]


def per_device(tf, sf, w, pairing):
    t_rows = tf.shape[0]
    rows = sf.shape[0]
    blocks = lax.axis_size("batch")
    peers = lax.axis_size("proto")
    me = lax.axis_index("batch").astype(jnp.int32).reshape(1)

    def swap(x, axis):
        return lax.all_to_all(x, axis, 0, 0)

    feats_f32 = lax.all_gather(turned(tf), "batch")
    pairs = pairing - me * t_rows
    onehot = (pairs[:, None] == jnp.arange(t_rows, dtype=jnp.int32)[None, :]).astype(BF16)
    gt = mm(sf, onehot, TN)
    wt, stats = student_stats(sf, tf, w, peers)
    stats = swap(stats, "proto")
    lse, shared = merge_stats(stats, gt, rows, blocks)
    shared = swap(shared, "batch")
    ds_prob, dw_prob = student_grads(sf, w, wt, lse, 0, None, peers)

    feats, offset, mass, dw_prob = first_iteration(feats_f32, shared, wt, dw_prob, peers)
    ds_prob, dw_prob = student_grads(sf, w, wt, lse, 1, (ds_prob, dw_prob), peers)
    for _ in range(ITERS - 2):
        offset, mass, dw_prob = next_iteration(feats, offset, swap(mass, "proto"), wt, dw_prob)
    dw_prob = lax.psum_scatter(dw_prob, "batch", scatter_dimension=0, tiled=True)
    offset, scale, taught, mass = last_iteration(
        me, feats, offset, swap(mass, "proto"), w, wt, gt
    )
    mass = swap(mass, "proto")
    loss, inverse, ds = after_iterations(me, mass, lse, taught, onehot, ds_prob, blocks)
    ds = swap(ds, "proto")
    far = 1
    while far < blocks:
        loss = loss + lax.ppermute(loss, "batch", [(i, i ^ far) for i in range(blocks)])
        far *= 2
    d_weight = dw_prob - weight_grad(
        feats, offset, inverse, wt, shared, scale, w.shape[1] * peers
    )
    return loss[0, 0] / (rows * blocks), jnp.sum(ds, axis=0), d_weight


def solution(mesh):
    placed = (P("batch", None), P("batch", None), P(None, "proto"), P("batch"))
    return jax.shard_map(
        per_device,
        mesh=mesh,
        in_specs=placed,
        out_specs=(P(), P(("batch", "proto"), None), P("batch", "proto")),
        check_vma=False,
    )
```

profile of v0, /device:TPU:1, one launch (start us, length us, event | category | flops | bytes accessed | tf_op | source)
XLA Modules:
  0.0 186.8 jit_solution(12994751943914739428)
XLA Ops:
  7.2 0.0 all-gather.3.cloned.1.call-start
  7.2 1.7 shard_map.67
  8.9 0.0 all-gather.3.cloned.1.call-update
  8.9 0.0 copy-start.5
  9.0 0.0 copy-start.6
  9.0 9.3 %shard_map.68 = (bf16[4096,256]{1,0:T(8,128)(2,1)}, f32[32,24,128]{2,1,0:T(8,128)}) custom-call(bf16[1024,256]{1,0:T(8,128)(2,1)} %sf_ref.5, bf16[256,256]{1,0:T(8,128)(2,1)} %tf_ref.3, bf16[256,4096]{1,0:T(8,128)(2,1)} %w_ref.7), custom_call_target="tpu_custom_call" | custom-call | flops 2684354560 | bytes 8388608 | tf_op jit(solution)/shard_map/pallas_call | solution.py:122
  18.2 8.6 %all-to-all-start = ((f32[32,24,128]{2,1,0:T(8,128)}), f32[32,24,128]{2,1,0:T(8,128)S(1)}, u32[]{:S(2)}, u32[]{:S(2)}) async-start(f32[32,24,128]{2,1,0:T(8,128)} %get-tuple-element.25), calls=%async_computation | async-start | bytes 786432 | tf_op jit(solution)/shard_map/all_to_all | solution.py:578
  26.8 0.0 copy-done.5
  26.8 0.0 copy-done.6
  26.9 1.2 convolution_bitcast_fusion.gt_ref
  28.1 9.0 %all-to-all-done.stats_ref = f32[32,24,128]{2,1,0:T(8,128)S(1)} async-done(((f32[32,24,128]{2,1,0:T(8,128)}), f32[32,24,128]{2,1,0:T(8,128)S(1)}, u32[]{:S(2)}, u32[]{:S(2)}) %all-to-all-start) | async-done | bytes 393248 | tf_op jit(solution)/shard_map/all_to_all | solution.py:578
  37.1 0.0 copy-start
  37.1 0.7 copy-done
  37.9 1.9 %shard_map.69 = (f32[8,128]{1,0:T(8,128)}, f32[8,40,256]{2,1,0:T(8,128)}) custom-call(f32[32,24,128]{2,1,0:T(8,128)} %copy-done, f32[256,256]{1,0:T(8,128)} %convolution_bitcast_fusion.gt_ref), custom_call_target="tpu_custom_call" | custom-call | flops 393216 | bytes 2097152 | tf_op jit(solution)/shard_map/pallas_call | solution.py:168
  39.8 8.2 %all-to-all-start.1 = ((f32[8,40,256]{2,1,0:T(8,128)}), f32[8,40,256]{2,1,0:T(8,128)S(1)}, u32[]{:S(2)}, u32[]{:S(2)}) async-start(f32[8,40,256]{2,1,0:T(8,128)} %get-tuple-element.26), calls=%async_computation.1 | async-start | bytes 655360 | tf_op jit(solution)/shard_map/all_to_all | solution.py:578
  47.9 9.8 %shard_map.70 = (f32[256,1024]{1,0:T(8,128)}, f32[256,4096]{1,0:T(8,128)}) custom-call(bf16[1024,256]{1,0:T(8,128)(2,1)} %sf_ref.5, bf16[256,4096]{1,0:T(8,128)(2,1)} %w_ref.7, bf16[4096,256]{1,0:T(8,128)(2,1)} %get-tuple-element.27.wt_ref, f32[8,128]{1,0:T(8,128)} %get-tuple-element.28.lse_ref), custom_call_target="tpu_custom_call" | custom-call | flops 8589934592 | bytes 6291456 | tf_op jit(solution)/shard_map/pallas_call | solution.py:225
  57.7 3.8 %all-to-all-done.1.shared_ref.sh_ref = f32[8,40,256]{2,1,0:T(8,128)S(1)} async-done(((f32[8,40,256]{2,1,0:T(8,128)}), f32[8,40,256]{2,1,0:T(8,128)S(1)}, u32[]{:S(2)}, u32[]{:S(2)}) %all-to-all-start.1) | async-done | bytes 327712 | tf_op jit(solution)/shard_map/all_to_all | solution.py:578
  61.6 0.0 copy-start.2
  61.6 0.8 copy-done.2
  62.3 11.5 %shard_map.71 = (bf16[8,256,256]{2,1,0:T(8,128)(2,1)}, f32[16,128]{1,0:T(8,128)}, f32[32,16,128]{2,1,0:T(8,128)}, f32[256,4096]{1,0:T(8,128)}) custom-call(f32[8,256,256]{2,1,0:T(8,128)} %bitcast.7, f32[8,40,256]{2,1,0:T(8,128)} %copy-done.2, bf16[4096,256]{1,0:T(8,128)(2,1)} %get-tuple-element.27.wt_ref, ...), custom_call_target="tpu_custom_call", output_to_operand_aliasing={{3}: (3, {})} | custom-call | flops 10737418240 | bytes 5242880 | tf_op jit(solution)/shard_map/pallas_call | solution.py:303
  73.8 5.9 %all-to-all-start.2 = ((f32[32,16,128]{2,1,0:T(8,128)}), f32[32,16,128]{2,1,0:T(8,128)S(1)}, u32[]{:S(2)}, u32[]{:S(2)}) async-start(f32[32,16,128]{2,1,0:T(8,128)} %get-tuple-element.32), calls=%async_computation.2 | async-start | bytes 524288 | tf_op jit(solution)/shard_map/all_to_all | solution.py:578
  79.7 0.0 reduce-scatter.2.cloned.1.call-start
  79.8 10.3 %shard_map.72 = (f32[32,32,256]{2,1,0:T(8,128)}, f32[256,4096]{1,0:T(8,128)}) custom-call(bf16[1024,256]{1,0:T(8,128)(2,1)} %sf_ref.5, bf16[256,4096]{1,0:T(8,128)(2,1)} %w_ref.7, bf16[4096,256]{1,0:T(8,128)(2,1)} %get-tuple-element.27.wt_ref, f32[8,128]{1,0:T(8,128)} %get-tuple-element.28.lse_ref, ...), custom_call_target="tpu_custom_call", output_to_operand_aliasing={{1}: (4, {})} | custom-call | flops 8589934592 | bytes 6291456 | tf_op jit(solution)/shard_map/pallas_call | solution.py:225
  90.1 0.0 all-to-all-done.2.recv_ref
  90.1 0.7 copy-done.3
  90.8 10.7 %shard_map.73 = (f32[16,128]{1,0:T(8,128)}, f32[32,16,128]{2,1,0:T(8,128)}, f32[256,4096]{1,0:T(8,128)}) custom-call(bf16[8,256,256]{2,1,0:T(8,128)(2,1)} %get-tuple-element.30.feat_ref, f32[16,128]{1,0:T(8,128)} %get-tuple-element.31.old_ref, f32[32,16,128]{2,1,0:T(8,128)} %copy-done.3, ...), custom_call_target="tpu_custom_call", output_to_operand_aliasing={{2}: (4, {})} | custom-call | flops 10737418240 | bytes 4194304 | tf_op jit(solution)/shard_map/pallas_call | solution.py:366
  101.6 0.0 reduce-scatter.2.cloned.1.call-update
  101.6 0.9 copy-done.4
  102.5 16.3 %all_to_all.30.recv_ref = f32[32,16,128]{2,1,0:T(8,128)} all-to-all(f32[32,16,128]{2,1,0:T(8,128)S(1)} %copy-done.4), channel_id=1, replica_groups=mesh['batch'=8,'proto'=32] {'proto'}, dimensions={0} | all-to-all | bytes 524288 | tf_op jit(solution)/shard_map/all_to_all | solution.py:578
  118.8 13.9 %shard_map.74 = (f32[16,128]{1,0:T(8,128)}, f32[4096,128]{1,0:T(8,128)}, f32[256,256]{1,0:T(8,128)}, f32[32,24,128]{2,1,0:T(8,128)}) custom-call(s32[1]{0:T(128)} %bitcast.me_ref, bf16[8,256,256]{2,1,0:T(8,128)(2,1)} %get-tuple-element.30.feat_ref, f32[16,128]{1,0:T(8,128)} %get-tuple-element.36.old_ref, f32[32,16,128]{2,1,0:T(8,128)} %all_to_all.30.recv_ref, ...), custom_call_target="tpu_custom_call" | custom-call | flops 5368709120 | bytes 8388608 | tf_op jit(solution)/shard_map/pallas_call | solution.py:440
  132.7 3.7 %all-to-all-start.4 = ((f32[32,24,128]{2,1,0:T(8,128)}), f32[32,24,128]{2,1,0:T(8,128)S(1)}, u32[]{:S(2)}, u32[]{:S(2)}) async-start(f32[32,24,128]{2,1,0:T(8,128)} %get-tuple-element.38), calls=%async_computation.4 | async-start | bytes 786432 | tf_op jit(solution)/shard_map/all_to_all | solution.py:578
  136.5 1.0 fusion.oh_ref
  137.5 9.4 %all-to-all-done.4.recv_ref = f32[32,24,128]{2,1,0:T(8,128)S(1)} async-done(((f32[32,24,128]{2,1,0:T(8,128)}), f32[32,24,128]{2,1,0:T(8,128)S(1)}, u32[]{:S(2)}, u32[]{:S(2)}) %all-to-all-start.4) | async-done | bytes 393248 | tf_op jit(solution)/shard_map/all_to_all | solution.py:578
  146.9 0.8 copy-done.1
  147.6 3.1 %shard_map.75 = (f32[8,128]{1,0:T(8,128)}, f32[16,128]{1,0:T(8,128)}, f32[32,32,256]{2,1,0:T(8,128)}) custom-call(s32[1]{0:T(128)} %bitcast.me_ref, f32[32,24,128]{2,1,0:T(8,128)} %copy-done.1, f32[8,128]{1,0:T(8,128)} %get-tuple-element.28.lse_ref, f32[256,256]{1,0:T(8,128)} %get-tuple-element.39.taught_ref, bf16[1024,256]{1,0:T(8,128)(2,1)} %fusion.oh_ref, ...), custom_call_target="tpu_custom_call" | custom-call | flops 268435456 | bytes 3145728 | tf_op jit(solution)/shard_map/pallas_call | solution.py:497
  150.7 1.0 collective-permute-start
  151.8 1.8 collective-permute-done
  153.5 0.7 add.11
  154.2 0.3 collective-permute-start.1
  154.5 4.5 %all-to-all-start.5 = ((f32[32,32,256]{2,1,0:T(8,128)}), f32[32,32,256]{2,1,0:T(8,128)S(1)}, u32[]{:S(2)}, u32[]{:S(2)}) async-start(f32[32,32,256]{2,1,0:T(8,128)} %get-tuple-element.42), calls=%async_computation.5 | async-start | bytes 2097152 | tf_op jit(solution)/shard_map/all_to_all | solution.py:578
  159.1 0.0 collective-permute-done.1
  159.1 3.2 %collective-permute-start.2 = (f32[8,128]{1,0:T(8,128)S(1)}, f32[8,128]{1,0:T(8,128)S(1)}, u32[]{:S(2)}, u32[]{:S(2)}) collective-permute-start(f32[8,128]{1,0:T(8,128)S(1)} %add.12), channel_id=1, source_target_pairs={{0,128},{32,160},{64,192},{96,224},{128,0},{160,32},{192,64},{224,... | collective-permute-start | bytes 12296 | tf_op jit(solution)/shard_map/ppermute | solution.py:603
  162.3 12.6 %shard_map.76 = f32[32,4096]{1,0:T(8,128)} custom-call(bf16[8,256,256]{2,1,0:T(8,128)(2,1)} %get-tuple-element.30.feat_ref, f32[16,128]{1,0:T(8,128)} %get-tuple-element.44.off_ref, f32[16,128]{1,0:T(8,128)} %get-tuple-element.45.inv_ref, bf16[4096,256]{1,0:T(8,128)(2,1)} %get-tuple-element.27.wt_ref, f32[8,40,256]{2,1,0:T(8,128)} %copy-done.2, ...), custom_call_target="tpu_custom_call" | custom-call | flops 12884901888 | bytes 6291456 | tf_op jit(solution)/shard_map/pallas_call | solution.py:546
  174.9 0.0 collective-permute-done.2
  174.9 0.5 slice.3
  176.1 0.0 all-to-all-done.5
  176.1 0.7 reduce_sum.9
  176.8 2.0 %sub.16 = f32[32,4096]{1,0:T(8,128)} subtract(f32[32,4096]{1,0:T(8,128)} %reduce-scatter.2.cloned.1.call-done, f32[32,4096]{1,0:T(8,128)} %shard_map.76) | non-fusion elementwise | flops 131072 | bytes 1572864 | tf_op jit(solution)/shard_map/sub | solution.py:605
  (8 shorter events, 0.0 us)
Async XLA Ops:
  7.2 54.4 %all-gather.3.cloned.1.call-start = ((), (), s32[]{:S(2)}) async-start(), calls=%async_computation.8 | async-start | bytes 2359296 | tf_op jit(solution)/shard_map/all_gather | solution.py:580
  8.9 17.9 %copy-start.5 = (s32[1024]{0:T(1024)S(1)}, s32[1024]{0:T(1024)}, u32[]{:S(2)}) copy-start(s32[1024]{0:T(1024)} %param.7) | copy-start | bytes 12292
  9.0 17.9 %copy-start.6 = (bf16[1024,256]{1,0:T(8,128)(2,1)S(1)}, bf16[1024,256]{1,0:T(8,128)(2,1)}, u32[]{:S(2)}) copy-start(bf16[1024,256]{1,0:T(8,128)(2,1)} %sf_ref.5) | copy-start | bytes 1572868
  18.2 18.9 %all-to-all-start = ((f32[32,24,128]{2,1,0:T(8,128)}), f32[32,24,128]{2,1,0:T(8,128)S(1)}, u32[]{:S(2)}, u32[]{:S(2)}) async-start(f32[32,24,128]{2,1,0:T(8,128)} %get-tuple-element.25), calls=%async_computation | async-start | bytes 786432 | tf_op jit(solution)/shard_map/all_to_all | solution.py:578
  37.1 0.7 copy-start
  39.8 21.8 %all-to-all-start.1 = ((f32[8,40,256]{2,1,0:T(8,128)}), f32[8,40,256]{2,1,0:T(8,128)S(1)}, u32[]{:S(2)}, u32[]{:S(2)}) async-start(f32[8,40,256]{2,1,0:T(8,128)} %get-tuple-element.26), calls=%async_computation.1 | async-start | bytes 655360 | tf_op jit(solution)/shard_map/all_to_all | solution.py:578
  61.6 0.8 copy-start.2
  73.8 16.3 %all-to-all-start.2 = ((f32[32,16,128]{2,1,0:T(8,128)}), f32[32,16,128]{2,1,0:T(8,128)S(1)}, u32[]{:S(2)}, u32[]{:S(2)}) async-start(f32[32,16,128]{2,1,0:T(8,128)} %get-tuple-element.32), calls=%async_computation.2 | async-start | bytes 524288 | tf_op jit(solution)/shard_map/all_to_all | solution.py:578
  79.7 97.0 %reduce-scatter.2.cloned.1.call-start = ((), (), s32[]{:S(2)}) async-start(), calls=%async_computation.7 | async-start | bytes 4718592 | tf_op jit(solution)/shard_map/reduce_scatter | solution.py:594
  90.1 0.7 copy-start.3
  101.6 0.9 copy-start.4
  132.7 14.1 %all-to-all-start.4 = ((f32[32,24,128]{2,1,0:T(8,128)}), f32[32,24,128]{2,1,0:T(8,128)S(1)}, u32[]{:S(2)}, u32[]{:S(2)}) async-start(f32[32,24,128]{2,1,0:T(8,128)} %get-tuple-element.38), calls=%async_computation.4 | async-start | bytes 786432 | tf_op jit(solution)/shard_map/all_to_all | solution.py:578
  146.9 0.8 copy-start.1
  150.7 2.8 %collective-permute-start = (f32[8,128]{1,0:T(8,128)}, f32[8,128]{1,0:T(8,128)S(1)}, u32[]{:S(2)}, u32[]{:S(2)}) collective-permute-start(f32[8,128]{1,0:T(8,128)} %get-tuple-element.41), channel_id=1, source_target_pairs={{0,32},{32,0},{64,96},{96,64},{128,160},{160,128},{192,224},{224,1... | collective-permute-start | bytes 12296 | tf_op jit(solution)/shard_map/ppermute | solution.py:603
  154.2 4.9 %collective-permute-start.1 = (f32[8,128]{1,0:T(8,128)S(1)}, f32[8,128]{1,0:T(8,128)S(1)}, u32[]{:S(2)}, u32[]{:S(2)}) collective-permute-start(f32[8,128]{1,0:T(8,128)S(1)} %add.11), channel_id=1, source_target_pairs={{0,64},{32,96},{64,0},{96,32},{128,192},{160,224},{192,128},{224,1... | collective-permute-start | bytes 12296 | tf_op jit(solution)/shard_map/ppermute | solution.py:603
  154.5 21.6 %all-to-all-start.5 = ((f32[32,32,256]{2,1,0:T(8,128)}), f32[32,32,256]{2,1,0:T(8,128)S(1)}, u32[]{:S(2)}, u32[]{:S(2)}) async-start(f32[32,32,256]{2,1,0:T(8,128)} %get-tuple-element.42), calls=%async_computation.5 | async-start | bytes 2097152 | tf_op jit(solution)/shard_map/all_to_all | solution.py:578
  159.1 15.8 %collective-permute-start.2 = (f32[8,128]{1,0:T(8,128)S(1)}, f32[8,128]{1,0:T(8,128)S(1)}, u32[]{:S(2)}, u32[]{:S(2)}) collective-permute-start(f32[8,128]{1,0:T(8,128)S(1)} %add.12), channel_id=1, source_target_pairs={{0,128},{32,160},{64,192},{96,224},{128,0},{160,32},{192,64},{224,... | collective-permute-start | bytes 12296 | tf_op jit(solution)/shard_map/ppermute | solution.py:603
Sparse Core Ops, SparseCore 0:
  9.8 41.1 all-gather.2
  101.7 52.5 reduce-scatter.1
where the time goes:
time: 188 us; the launch traced here: 187 us
  Pallas kernels  84.8 us (45%)
  starting transfers between devices  35.6 us (19%)
  waiting for transfers between devices  24.1 us (13%)
  blocking collectives  16.3 us (9%)
  between operations  15.9 us (8%)
  local copies, waits for them, and re-layouts  4.43 us (2%)
  other arithmetic  4.42 us (2%)
    all_to_all x5, starting transfers between devices, swap(): return lax.all_to_all(x, axis, 0, 0)  30.9 us
    all_to_all x5, waiting for transfers between devices, swap(): return lax.all_to_all(x, axis, 0, 0)  22.3 us
    pallas_call x2, Pallas kernels, student_grads(): call(body, steps, in_specs, [whole(ds_shape), pl.BlockSpec((width, S_CHUN...  20.1 us
    all_to_all x1, blocking collectives, swap(): return lax.all_to_all(x, axis, 0, 0)  16.3 us
    pallas_call x1, Pallas kernels, last_iteration(): call(body, steps, [pl.BlockSpec(memory_space=pltpu.SMEM), whole(feats.sha...  13.9 us
    pallas_call x1, Pallas kernels, weight_grad(): call(body, steps, [whole(feats.shape), whole(offset_packed.shape), whole(...  12.6 us
    pallas_call x1, Pallas kernels, first_iteration(): call(body, steps, [whole(feats_f32.shape), whole(shared.shape), pl.BlockS...  11.5 us
    pallas_call x1, Pallas kernels, next_iteration(): call(body, steps, [whole(feats.shape), whole(old.shape), whole(received.s...  10.7 us
  transfers between devices with their start and end apart: 10, of which 4 were waited for; matrix products, arithmetic and copies ran while one was open for 2% of the time, Pallas kernels for 33%

commit v1 on v0

--- a/solution.py
+++ b/solution.py
@@ -21,7 +21,7 @@
 NN = (((1,), (0,)), ((), ()))
 NT = (((1,), (1,)), ((), ()))
 TN = (((0,), (0,)), ((), ()))
-VMEM_LIMIT = 60 * 1024 * 1024
+VMEM_LIMIT = 56 * 1024 * 1024
 
 
 def mm(a, b, dims):
@@ -181,8 +181,10 @@
 def student_grads(sf, w, wt, lse, half, before, peers):
     rows, width = sf.shape
     columns = w.shape[1]
-    steps = columns // S_CHUNK // 2
-    first = half * steps
+    all_steps = columns // S_CHUNK
+    cut = (5 * all_steps) // 8
+    steps = all_steps - cut if half else cut
+    first = half * cut
     s_rows = rows // LANES
 
     def body(sf_ref, w_ref, wt_ref, lse_ref, *rest):
@@ -233,7 +235,7 @@
             pltpu.VMEM((width, rows), BF16),
             pltpu.VMEM((width, rows), F32),
         ],
-        8 * columns * width * rows,
+        16 * columns * width * rows * steps // all_steps,
         columns * rows // 2,
         6 * 2**20,
         {4: 1} if half else None,
@@ -287,7 +289,7 @@
         def _():
             feat_out[...] = feat_ref[...].astype(BF16)
             for i in range(blocks):
-                row = shared_ref[i, share : share + 1, :]
+                row = shared_ref[i, 0:1, :]
                 offset[i : i + 1, :] = row
                 put_rows(off_out, i * tr, row)
             mass[...] = jnp.zeros_like(mass)
@@ -305,7 +307,7 @@
         steps,
         [
             whole(feats_f32.shape),
-            whole(shared.shape),
+            pl.BlockSpec((blocks, 8, t_rows), lambda c: (0, share // 8, 0)),
             pl.BlockSpec((T_CHUNK, width), lambda c: (c, 0)),
             pl.BlockSpec(memory_space=pl.ANY),
         ],
@@ -334,10 +336,9 @@
     )(feats_f32, shared, wt, passed)
 
 
-def next_iteration(feats, old, received, wt, passed):
+def next_iteration(feats, old, received, wt, passed, peers):
     blocks, width, t_rows = feats.shape
     columns = wt.shape[0]
-    peers = received.shape[0]
     steps = columns // T_CHUNK
     tr = t_rows // LANES
     total_t = blocks * t_rows
@@ -350,7 +351,7 @@
 
         @pl.when(step == 0)
         def _():
-            packed = old_ref[...] + jnp.log2(total_t * jnp.sum(recv_ref[...], axis=0))
+            packed = old_ref[...] + jnp.log2(total_t * recv_ref[...])
             off_out[...] = packed
             fill_offsets(offset, packed, blocks, tr)
             mass[...] = jnp.zeros_like(mass)
@@ -392,10 +393,9 @@
     )(feats, old, received, wt, passed)
 
 
-def last_iteration(me, feats, old, received, w, wt, gt):
+def last_iteration(me, feats, old, received, w, wt, gt, peers):
     blocks, width, t_rows = feats.shape
     columns = wt.shape[0]
-    peers = received.shape[0]
     steps = columns // T_CHUNK
     tr = t_rows // LANES
     total_t = blocks * t_rows
@@ -409,7 +409,7 @@
 
         @pl.when(step == 0)
         def _():
-            packed = old_ref[...] + jnp.log2(total_t * jnp.sum(recv_ref[...], axis=0))
+            packed = old_ref[...] + jnp.log2(total_t * recv_ref[...])
             off_out[...] = packed
             fill_offsets(offset, packed, blocks, tr)
             mass[...] = jnp.zeros_like(mass)
@@ -477,17 +477,17 @@
     )(me, feats, old, received, w, wt, gt)
 
 
-def after_iterations(me, received, lse, taught, onehot, ds_prob, blocks):
+def after_iterations(me, received, lse, taught, onehot, ds_prob, near, blocks):
     width, t_rows = taught.shape
     tr = t_rows // LANES
     n = blocks * tr
 
-    def body(me_ref, recv_ref, lse_ref, taught_ref, oh_ref, prob_ref, part_ref, inv_ref, ds_ref):
-        total = jnp.sum(recv_ref[...], axis=0)
-        inv_ref[...] = 1.0 / total[:n]
-        start = me_ref[0] * tr
-        inverse = 1.0 / jnp.sum(recv_ref[:, pl.ds(start, tr), :], axis=0)
-        product = jnp.sum(total[n : n + tr] * inverse) / STUDENT_TEMP
+    def body(
+        me_ref, recv_ref, lse_ref, taught_ref, oh_ref, prob_ref, _, part_ref, inv_ref, ds_ref
+    ):
+        inv_ref[...] = 1.0 / recv_ref[:n, :]
+        inverse = inv_ref[pl.ds(me_ref[0] * tr, tr), :]
+        product = jnp.sum(recv_ref[n : n + tr, :] * inverse) / STUDENT_TEMP
         part_ref[...] = jnp.full(part_ref.shape, jnp.sum(lse_ref[...]) / LOG2E - product, F32)
         row = jnp.concatenate([inverse[i : i + 1, :] for i in range(tr)], axis=1)
         high, low = halves(taught_ref[...] * row / STUDENT_TEMP)
@@ -504,6 +504,7 @@
             whole(taught.shape),
             whole(onehot.shape),
             whole(ds_prob.shape),
+            pl.BlockSpec(memory_space=pl.ANY),
         ],
         [whole((8, LANES)), whole((n, LANES)), whole(ds_prob.shape)],
         [struct((8, LANES)), struct((n, LANES)), struct(ds_prob.shape)],
@@ -511,36 +512,83 @@
         4 * onehot.size * width,
         1024,
         3 * 2**20,
-    )(me, received, lse, taught, onehot, ds_prob)
-
-
-def weight_grad(feats, offset_packed, inverse, wt, shared, scale, all_columns):
+    )(me, received, lse, taught, onehot, ds_prob, near)
+
+
+def middle_of(scale_ref, all_columns, total_t, tr):
+    middle = 1.0 / (all_columns * total_t * scale_ref)
+    return middle, jnp.concatenate([middle] * tr, axis=1)
+
+
+def early_expos(feats, offset_packed, wt, scale, all_columns):
     blocks, width, t_rows = feats.shape
     columns = wt.shape[0]
+    half = T_CHUNK // 2
+    steps = columns // T_CHUNK
+    tr = t_rows // LANES
+
+    def body(feat_ref, off_ref, wt_ref, scale_ref, out_ref, offset):
+        @pl.when(pl.program_id(0) == 0)
+        def _():
+            fill_offsets(offset, off_ref[...], blocks, tr)
+
+        _, wide = middle_of(scale_ref[...], all_columns, blocks * t_rows, tr)
+        for i in range(blocks):
+            scores = mm(wt_ref[...], feat_ref[i], NN)
+            expo = jnp.exp2(scores * T_SCALE - offset[i : i + 1, :])
+            out_ref[i] = (expo - wide).astype(BF16)
+
+    return call(
+        body,
+        steps,
+        [
+            whole(feats.shape),
+            whole(offset_packed.shape),
+            pl.BlockSpec((half, width), lambda c: (2 * c, 0)),
+            pl.BlockSpec((half, LANES), lambda c: (2 * c, 0)),
+        ],
+        [pl.BlockSpec((blocks, half, t_rows), lambda c: (0, c, 0))],
+        [struct((blocks, columns // 2, t_rows), BF16)],
+        [pltpu.VMEM((max(blocks, 8), t_rows), F32)],
+        2 * columns * width * t_rows * blocks,
+        columns * t_rows * blocks // 2,
+        10 * 2**20,
+    )(feats, offset_packed, wt, scale)[0]
+
+
+def weight_grad(feats, offset_packed, inverse, wt, shared, scale, near, all_columns):
+    blocks, width, t_rows = feats.shape
+    columns = wt.shape[0]
+    half = T_CHUNK // 2
     steps = columns // T_CHUNK
     tr = t_rows // LANES
     share = shared.shape[1] - 8
 
-    def body(feat_ref, off_ref, inv_ref, wt_ref, sh_ref, scale_ref, out_ref, offset, g, g_sum):
+    def body(
+        feat_ref, off_ref, inv_ref, wt_ref, sh_ref, scale_ref, near_ref,
+        out_ref, offset, factor, g, g_sum,
+    ):
         @pl.when(pl.program_id(0) == 0)
         def _():
-            fill_offsets(offset, off_ref[...] - jnp.log2(inv_ref[...]), blocks, tr)
+            fill_offsets(offset, off_ref[...], blocks, tr)
+            fill_offsets(factor, inv_ref[...], blocks, tr)
             total = jnp.zeros((8, LANES), F32)
             for i in range(blocks):
-                high, low = halves(sh_ref[i, :share, :] / STUDENT_TEMP)
+                high, low = halves(sh_ref[i, :share, :] * factor[i : i + 1, :] / STUDENT_TEMP)
                 part = jnp.concatenate([high, low, jnp.zeros((LANES - 2 * share, t_rows), BF16)])
                 g[i] = part
                 total += mm(jnp.ones((8, t_rows), BF16), part, NT)
             g_sum[...] = total
 
-        middle = 1.0 / (all_columns * scale_ref[...])
-        wide = jnp.concatenate([middle] * tr, axis=1)
-        acc = middle * g_sum[0:1, :]
+        middle, wide = middle_of(scale_ref[...], all_columns, blocks * t_rows, tr)
+        early = middle[:half] * g_sum[0:1, :]
+        late = middle[half:] * g_sum[0:1, :]
         for i in range(blocks):
             scores = mm(wt_ref[...], feat_ref[i], NN)
             expo = jnp.exp2(scores * T_SCALE - offset[i : i + 1, :])
-            acc += mm((expo - wide).astype(BF16), g[i], NT)
-        out = (acc * scale_ref[...]).T
+            late += mm((expo - wide[half:]).astype(BF16), g[i], NT)
+            early += mm(near_ref[i], g[i], NT)
+        out = (jnp.concatenate([early, late]) * scale_ref[...]).T
         out_ref[...] = out[:share] + out[share : 2 * share]
 
     return call(
@@ -550,21 +598,23 @@
             whole(feats.shape),
             whole(offset_packed.shape),
             whole(inverse.shape),
-            pl.BlockSpec((T_CHUNK, width), lambda c: (c, 0)),
+            pl.BlockSpec((half, width), lambda c: (2 * c + 1, 0)),
             whole(shared.shape),
             pl.BlockSpec((T_CHUNK, LANES), lambda c: (c, 0)),
+            pl.BlockSpec((blocks, half, t_rows), lambda c: (0, c, 0)),
         ],
         [pl.BlockSpec((share, T_CHUNK), lambda c: (0, c))],
         [struct((share, columns))],
         [
+            pltpu.VMEM((max(blocks, 8), t_rows), F32),
             pltpu.VMEM((max(blocks, 8), t_rows), F32),
             pltpu.VMEM((blocks, LANES, t_rows), BF16),
             pltpu.VMEM((8, LANES), F32),
         ],
         6 * columns * width * t_rows * blocks,
         columns * t_rows * blocks,
-        6 * 2**20,
-    )(feats, offset_packed, inverse, wt, shared, scale)[0]
+        14 * 2**20,
+    )(feats, offset_packed, inverse, wt, shared, scale, near)[0]
 
 
 def per_device(tf, sf, w, pairing):
@@ -590,20 +640,24 @@
     feats, offset, mass, dw_prob = first_iteration(feats_f32, shared, wt, dw_prob, peers)
     ds_prob, dw_prob = student_grads(sf, w, wt, lse, 1, (ds_prob, dw_prob), peers)
     for _ in range(ITERS - 2):
-        offset, mass, dw_prob = next_iteration(feats, offset, swap(mass, "proto"), wt, dw_prob)
+        mass = jnp.sum(swap(mass, "proto"), axis=0)
+        offset, mass, dw_prob = next_iteration(feats, offset, mass, wt, dw_prob, peers)
     dw_prob = lax.psum_scatter(dw_prob, "batch", scatter_dimension=0, tiled=True)
-    offset, scale, taught, mass = last_iteration(
-        me, feats, offset, swap(mass, "proto"), w, wt, gt
+    mass = jnp.sum(swap(mass, "proto"), axis=0)
+    offset, scale, taught, mass = last_iteration(me, feats, offset, mass, w, wt, gt, peers)
+    all_columns = w.shape[1] * peers
+    near = early_expos(feats, offset, wt, scale, all_columns)
+    mass = jnp.sum(swap(mass, "proto"), axis=0)
+    loss, inverse, ds = after_iterations(
+        me, mass, lse, taught, onehot, ds_prob, near, blocks
     )
-    mass = swap(mass, "proto")
-    loss, inverse, ds = after_iterations(me, mass, lse, taught, onehot, ds_prob, blocks)
     ds = swap(ds, "proto")
     far = 1
     while far < blocks:
         loss = loss + lax.ppermute(loss, "batch", [(i, i ^ far) for i in range(blocks)])
         far *= 2
     d_weight = dw_prob - weight_grad(
-        feats, offset, inverse, wt, shared, scale, w.shape[1] * peers
+        feats, offset, inverse, wt, shared, scale, near, all_columns
     )
     return loss[0, 0] / (rows * blocks), jnp.sum(ds, axis=0), d_weight
 

time: 188 us -> 186 us (0.989)
  blocking collectives: 16.3 us -> 0 us
  starting transfers between devices: 35.6 us -> 43.1 us
  Pallas kernels: 84.8 us -> 90.3 us
  local copies, waits for them, and re-layouts: 4.43 us -> 1.99 us
  waiting for transfers between devices: 24.1 us -> 26.3 us
  other arithmetic: 4.42 us -> 6.31 us
    all_to_all x1 -> x0, blocking collectives: 16.3 us -> none  [swap(): return lax.all_to_all(x, axis, 0, 0)]
    all_to_all x5 -> x6, starting transfers between devices: 30.9 us -> 38.8 us  [swap(): return lax.all_to_all(x, axis, 0, 0)]
    pallas_call x1 -> x2, Pallas kernels: 11.5 us -> 18.7 us  [the longest x1 11.5 us: first_iteration(): call(body, steps, [whole(feats_f32.shape), pl.BlockSpec((blocks, 8, t_row...]
    unnamed x14 -> x8, local copies, waits for them, and re-layouts: 3.91 us -> 1.48 us
    reduce_sum x0 -> x3, other arithmetic: none -> 1.9 us  [per_device(): mass = jnp.sum(swap(mass, 'proto'), axis=0)]
    all_to_all x5 -> x6, waiting for transfers between devices: 22.3 us -> 24.1 us  [swap(): return lax.all_to_all(x, axis, 0, 0)]
  transfers between devices with their start and end apart: 10 -> 11, of which waited for: 4 -> 7; matrix products, arithmetic and copies ran while one was open for 2% -> 3% of each run, Pallas kernels for 33% -> 36%
where the time goes in v1:
time: 186 us; the launch traced here: 185 us
  Pallas kernels  90.3 us (49%)
  starting transfers between devices  43.1 us (23%)
  waiting for transfers between devices  26.3 us (14%)
  between operations  15.9 us (9%)
  other arithmetic  6.31 us (3%)
  local copies, waits for them, and re-layouts  1.99 us (1%)
    all_to_all x6, starting transfers between devices, swap(): return lax.all_to_all(x, axis, 0, 0)  38.8 us
    all_to_all x6, waiting for transfers between devices, swap(): return lax.all_to_all(x, axis, 0, 0)  24.1 us
    pallas_call x2, Pallas kernels, student_grads(): call(body, steps, in_specs, [whole(ds_shape), pl.BlockSpec((width, S_CHUN...  20.1 us
    pallas_call x1, Pallas kernels, last_iteration(): call(body, steps, [pl.BlockSpec(memory_space=pltpu.SMEM), whole(feats.sha...  13.9 us
    pallas_call x1, Pallas kernels, first_iteration(): call(body, steps, [whole(feats_f32.shape), pl.BlockSpec((blocks, 8, t_row...  11.5 us
    pallas_call x1, Pallas kernels, weight_grad(): call(body, steps, [whole(feats.shape), whole(offset_packed.shape), whole(...  11.1 us
    pallas_call x1, Pallas kernels, next_iteration(): call(body, steps, [whole(feats.shape), whole(old.shape), whole(received.s...  10.7 us
    pallas_call x1, Pallas kernels, student_stats(): call(body, steps, [whole(sf.shape), whole(tf.shape), pl.BlockSpec((width,...  9.26 us
  transfers between devices with their start and end apart: 11, of which 7 were waited for; matrix products, arithmetic and copies ran while one was open for 3% of the time, Pallas kernels for 36%

profile of v1, /device:TPU:1, one launch (start us, length us, event | category | flops | bytes accessed | tf_op | source)
XLA Modules:
  0.0 185.1 jit_solution(2666095247887072713)
XLA Ops:
  7.2 0.0 all-gather.3.cloned.1.call-start
  7.2 1.7 shard_map.67
  8.9 0.0 all-gather.3.cloned.1.call-update
  9.0 0.0 copy-start.2
  9.0 0.0 copy-start.3
  9.0 9.3 %shard_map.68 = (bf16[4096,256]{1,0:T(8,128)(2,1)}, f32[32,24,128]{2,1,0:T(8,128)}) custom-call(bf16[1024,256]{1,0:T(8,128)(2,1)} %sf_ref.5, bf16[256,256]{1,0:T(8,128)(2,1)} %tf_ref.3, bf16[256,4096]{1,0:T(8,128)(2,1)} %w_ref.7), custom_call_target="tpu_custom_call" | custom-call | flops 2684354560 | bytes 8388608 | tf_op jit(solution)/shard_map/pallas_call | solution.py:122
  18.2 8.6 %all-to-all-start = ((f32[32,24,128]{2,1,0:T(8,128)}), f32[32,24,128]{2,1,0:T(8,128)S(1)}, u32[]{:S(2)}, u32[]{:S(2)}) async-start(f32[32,24,128]{2,1,0:T(8,128)} %get-tuple-element.25), calls=%async_computation | async-start | bytes 786432 | tf_op jit(solution)/shard_map/all_to_all | solution.py:628
  26.8 0.0 copy-done.2
  26.9 0.0 copy-done.3
  26.9 1.3 convolution_bitcast_fusion.gt_ref
  28.1 9.0 %all-to-all-done.stats_ref = f32[32,24,128]{2,1,0:T(8,128)S(1)} async-done(((f32[32,24,128]{2,1,0:T(8,128)}), f32[32,24,128]{2,1,0:T(8,128)S(1)}, u32[]{:S(2)}, u32[]{:S(2)}) %all-to-all-start) | async-done | bytes 393248 | tf_op jit(solution)/shard_map/all_to_all | solution.py:628
  37.1 0.7 copy-done
  37.9 1.9 %shard_map.69 = (f32[8,128]{1,0:T(8,128)}, f32[8,40,256]{2,1,0:T(8,128)}) custom-call(f32[32,24,128]{2,1,0:T(8,128)} %copy-done, f32[256,256]{1,0:T(8,128)} %convolution_bitcast_fusion.gt_ref), custom_call_target="tpu_custom_call" | custom-call | flops 393216 | bytes 2097152 | tf_op jit(solution)/shard_map/pallas_call | solution.py:168
  39.7 8.2 %all-to-all-start.1 = ((f32[8,40,256]{2,1,0:T(8,128)}), f32[8,40,256]{2,1,0:T(8,128)S(1)}, u32[]{:S(2)}, u32[]{:S(2)}) async-start(f32[8,40,256]{2,1,0:T(8,128)} %get-tuple-element.26), calls=%async_computation.1 | async-start | bytes 655360 | tf_op jit(solution)/shard_map/all_to_all | solution.py:628
  47.9 11.5 %shard_map.70 = (f32[256,1024]{1,0:T(8,128)}, f32[256,4096]{1,0:T(8,128)}) custom-call(bf16[1024,256]{1,0:T(8,128)(2,1)} %sf_ref.5, bf16[256,4096]{1,0:T(8,128)(2,1)} %w_ref.7, bf16[4096,256]{1,0:T(8,128)(2,1)} %get-tuple-element.27.wt_ref, f32[8,128]{1,0:T(8,128)} %get-tuple-element.28.lse_ref), custom_call_target="tpu_custom_call" | custom-call | flops 10737418240 | bytes 6291456 | tf_op jit(solution)/shard_map/pallas_call | solution.py:227
  59.4 2.1 %all-to-all-done.1.shared_ref.sh_ref = f32[8,40,256]{2,1,0:T(8,128)S(1)} async-done(((f32[8,40,256]{2,1,0:T(8,128)}), f32[8,40,256]{2,1,0:T(8,128)S(1)}, u32[]{:S(2)}, u32[]{:S(2)}) %all-to-all-start.1) | async-done | bytes 327712 | tf_op jit(solution)/shard_map/all_to_all | solution.py:628
  61.5 0.7 copy-done.1
  62.2 11.5 %shard_map.71 = (bf16[8,256,256]{2,1,0:T(8,128)(2,1)}, f32[16,128]{1,0:T(8,128)}, f32[32,16,128]{2,1,0:T(8,128)}, f32[256,4096]{1,0:T(8,128)}) custom-call(f32[8,256,256]{2,1,0:T(8,128)} %bitcast.7, f32[8,40,256]{2,1,0:T(8,128)} %copy-done.1, bf16[4096,256]{1,0:T(8,128)(2,1)} %get-tuple-element.27.wt_ref, ...), custom_call_target="tpu_custom_call", output_to_operand_aliasing={{3}: (3, {})} | custom-call | flops 10737418240 | bytes 5242880 | tf_op jit(solution)/shard_map/pallas_call | solution.py:305
  73.7 5.9 %all-to-all-start.2 = ((f32[32,16,128]{2,1,0:T(8,128)}), f32[32,16,128]{2,1,0:T(8,128)S(1)}, u32[]{:S(2)}, u32[]{:S(2)}) async-start(f32[32,16,128]{2,1,0:T(8,128)} %get-tuple-element.32), calls=%async_computation.2 | async-start | bytes 524288 | tf_op jit(solution)/shard_map/all_to_all | solution.py:628
  79.7 0.0 reduce-scatter.2.cloned.1.call-start
  79.7 8.6 %shard_map.72 = (f32[32,32,256]{2,1,0:T(8,128)}, f32[256,4096]{1,0:T(8,128)}) custom-call(bf16[1024,256]{1,0:T(8,128)(2,1)} %sf_ref.5, bf16[256,4096]{1,0:T(8,128)(2,1)} %w_ref.7, bf16[4096,256]{1,0:T(8,128)(2,1)} %get-tuple-element.27.wt_ref, f32[8,128]{1,0:T(8,128)} %get-tuple-element.28.lse_ref, ...), custom_call_target="tpu_custom_call", output_to_operand_aliasing={{1}: (4, {})} | custom-call | flops 6442450944 | bytes 6291456 | tf_op jit(solution)/shard_map/pallas_call | solution.py:227
  88.3 0.4 all-to-all-done.2
  88.7 0.6 reduce_sum.36.recv_ref
  89.3 10.7 %shard_map.73 = (f32[16,128]{1,0:T(8,128)}, f32[32,16,128]{2,1,0:T(8,128)}, f32[256,4096]{1,0:T(8,128)}) custom-call(bf16[8,256,256]{2,1,0:T(8,128)(2,1)} %get-tuple-element.30.feat_ref, f32[16,128]{1,0:T(8,128)} %get-tuple-element.31.old_ref, f32[16,128]{1,0:T(8,128)} %reduce_sum.36.recv_ref, ...), custom_call_target="tpu_custom_call", output_to_operand_aliasing={{2}: (4, {})} | custom-call | flops 10737418240 | bytes 4194304 | tf_op jit(solution)/shard_map/pallas_call | solution.py:367
  100.0 0.0 reduce-scatter.2.cloned.1.call-update
  100.0 7.0 %all-to-all-start.3 = ((f32[32,16,128]{2,1,0:T(8,128)}), f32[32,16,128]{2,1,0:T(8,128)S(1)}, u32[]{:S(2)}, u32[]{:S(2)}) async-start(f32[32,16,128]{2,1,0:T(8,128)} %get-tuple-element.37), calls=%async_computation.3 | async-start | bytes 524288 | tf_op jit(solution)/shard_map/all_to_all | solution.py:628
  107.1 1.0 fusion.oh_ref
  108.1 8.0 %all-to-all-done.3 = f32[32,16,128]{2,1,0:T(8,128)S(1)} async-done(((f32[32,16,128]{2,1,0:T(8,128)}), f32[32,16,128]{2,1,0:T(8,128)S(1)}, u32[]{:S(2)}, u32[]{:S(2)}) %all-to-all-start.3) | async-done | bytes 262176 | tf_op jit(solution)/shard_map/all_to_all | solution.py:628
  116.1 0.6 reduce_sum.37.recv_ref
  116.7 13.9 %shard_map.74 = (f32[16,128]{1,0:T(8,128)}, f32[4096,128]{1,0:T(8,128)}, f32[256,256]{1,0:T(8,128)}, f32[32,24,128]{2,1,0:T(8,128)}) custom-call(s32[1]{0:T(128)} %bitcast.me_ref, bf16[8,256,256]{2,1,0:T(8,128)(2,1)} %get-tuple-element.30.feat_ref, f32[16,128]{1,0:T(8,128)} %get-tuple-element.36.old_ref, f32[16,128]{1,0:T(8,128)} %reduce_sum.37.recv_ref, ...), custom_call_target="tpu_custom_call" | custom-call | flops 5368709120 | bytes 8388608 | tf_op jit(solution)/shard_map/pallas_call | solution.py:440
  130.6 3.7 %all-to-all-start.4 = ((f32[32,24,128]{2,1,0:T(8,128)}), f32[32,24,128]{2,1,0:T(8,128)S(1)}, u32[]{:S(2)}, u32[]{:S(2)}) async-start(f32[32,24,128]{2,1,0:T(8,128)} %get-tuple-element.38), calls=%async_computation.4 | async-start | bytes 786432 | tf_op jit(solution)/shard_map/all_to_all | solution.py:628
  134.3 7.2 %shard_map.75._.near_ref = bf16[8,2048,256]{2,1,0:T(8,128)(2,1)} custom-call(bf16[8,256,256]{2,1,0:T(8,128)(2,1)} %get-tuple-element.30.feat_ref, f32[16,128]{1,0:T(8,128)} %get-tuple-element.41.off_ref, bf16[4096,256]{1,0:T(8,128)(2,1)} %get-tuple-element.27.wt_ref, f32[4096,128]{1,0:T(8,128)} %get-tuple-element.42.scale_ref), custom_call_target="tpu_custom_call" | custom-call | flops 4294967296 | bytes 10485760 | tf_op jit(solution)/shard_map/pallas_call | solution.py:541
  141.5 3.2 %all-to-all-done.4 = f32[32,24,128]{2,1,0:T(8,128)S(1)} async-done(((f32[32,24,128]{2,1,0:T(8,128)}), f32[32,24,128]{2,1,0:T(8,128)S(1)}, u32[]{:S(2)}, u32[]{:S(2)}) %all-to-all-start.4) | async-done | bytes 393248 | tf_op jit(solution)/shard_map/all_to_all | solution.py:628
  144.7 0.6 reduce_sum.38.recv_ref
  145.4 3.0 %shard_map.76 = (f32[8,128]{1,0:T(8,128)}, f32[16,128]{1,0:T(8,128)}, f32[32,32,256]{2,1,0:T(8,128)}) custom-call(s32[1]{0:T(128)} %bitcast.me_ref, f32[24,128]{1,0:T(8,128)} %reduce_sum.38.recv_ref, f32[8,128]{1,0:T(8,128)} %get-tuple-element.28.lse_ref, f32[256,256]{1,0:T(8,128)} %get-tuple-element.39.taught_ref, bf16[1024,256]{1,0:T(8,128)(2,1)} %fusion.oh_ref, ...), custom_call_target="tpu_custom_call" | custom-call | flops 268435456 | bytes 3145728 | tf_op jit(solution)/shard_map/pallas_call | solution.py:497
  148.3 1.0 collective-permute-start
  149.3 2.1 %collective-permute-done = f32[8,128]{1,0:T(8,128)S(1)} collective-permute-done((f32[8,128]{1,0:T(8,128)}, f32[8,128]{1,0:T(8,128)S(1)}, u32[]{:S(2)}, u32[]{:S(2)}) %collective-permute-start) | collective-permute-done | bytes 4128 | tf_op jit(solution)/shard_map/ppermute | solution.py:657
  151.4 0.7 add.11
  152.1 0.1 collective-permute-start.1
  152.1 5.4 %all-to-all-start.5 = ((f32[32,32,256]{2,1,0:T(8,128)}), f32[32,32,256]{2,1,0:T(8,128)S(1)}, u32[]{:S(2)}, u32[]{:S(2)}) async-start(f32[32,32,256]{2,1,0:T(8,128)} %get-tuple-element.44), calls=%async_computation.5 | async-start | bytes 2097152 | tf_op jit(solution)/shard_map/all_to_all | solution.py:628
  157.5 0.0 collective-permute-done.1
  157.5 3.1 %collective-permute-start.2 = (f32[8,128]{1,0:T(8,128)S(1)}, f32[8,128]{1,0:T(8,128)S(1)}, u32[]{:S(2)}, u32[]{:S(2)}) collective-permute-start(f32[8,128]{1,0:T(8,128)S(1)} %add.12), channel_id=1, source_target_pairs={{0,128},{32,160},{64,192},{96,224},{128,0},{160,32},{192,64},{224,... | collective-permute-start | bytes 12296 | tf_op jit(solution)/shard_map/ppermute | solution.py:657
  160.7 11.1 %shard_map.77 = f32[32,4096]{1,0:T(8,128)} custom-call(bf16[8,256,256]{2,1,0:T(8,128)(2,1)} %get-tuple-element.30.feat_ref, f32[16,128]{1,0:T(8,128)} %get-tuple-element.41.off_ref, f32[16,128]{1,0:T(8,128)} %get-tuple-element.46.inv_ref, bf16[4096,256]{1,0:T(8,128)(2,1)} %get-tuple-element.27.wt_ref, f32[8,40,256]{2,1,0:T(8,128)} %copy-done.1, ...), custom_call_target="tpu_custom_call" | custom-call | flops 12884901888 | bytes 14680064 | tf_op jit(solution)/shard_map/pallas_call | solution.py:594
  171.7 0.0 collective-permute-done.2
  171.7 0.5 slice.3
  172.9 1.5 all-to-all-done.5
  174.4 0.7 reduce_sum.39
  175.1 2.0 %sub.16 = f32[32,4096]{1,0:T(8,128)} subtract(f32[32,4096]{1,0:T(8,128)} %reduce-scatter.2.cloned.1.call-done, f32[32,4096]{1,0:T(8,128)} %shard_map.77) | non-fusion elementwise | flops 131072 | bytes 1572864 | tf_op jit(solution)/shard_map/sub | solution.py:659
  (7 shorter events, 0.0 us)
Async XLA Ops:
  7.2 54.3 %all-gather.3.cloned.1.call-start = ((), (), s32[]{:S(2)}) async-start(), calls=%async_computation.8 | async-start | bytes 2359296 | tf_op jit(solution)/shard_map/all_gather | solution.py:630
  9.0 17.9 %copy-start.2 = (s32[1024]{0:T(1024)S(1)}, s32[1024]{0:T(1024)}, u32[]{:S(2)}) copy-start(s32[1024]{0:T(1024)} %param.7) | copy-start | bytes 12292
  9.0 17.9 %copy-start.3 = (bf16[1024,256]{1,0:T(8,128)(2,1)S(1)}, bf16[1024,256]{1,0:T(8,128)(2,1)}, u32[]{:S(2)}) copy-start(bf16[1024,256]{1,0:T(8,128)(2,1)} %sf_ref.5) | copy-start | bytes 1572868
  18.2 18.9 %all-to-all-start = ((f32[32,24,128]{2,1,0:T(8,128)}), f32[32,24,128]{2,1,0:T(8,128)S(1)}, u32[]{:S(2)}, u32[]{:S(2)}) async-start(f32[32,24,128]{2,1,0:T(8,128)} %get-tuple-element.25), calls=%async_computation | async-start | bytes 786432 | tf_op jit(solution)/shard_map/all_to_all | solution.py:628
  37.1 0.7 copy-start
  39.7 21.8 %all-to-all-start.1 = ((f32[8,40,256]{2,1,0:T(8,128)}), f32[8,40,256]{2,1,0:T(8,128)S(1)}, u32[]{:S(2)}, u32[]{:S(2)}) async-start(f32[8,40,256]{2,1,0:T(8,128)} %get-tuple-element.26), calls=%async_computation.1 | async-start | bytes 655360 | tf_op jit(solution)/shard_map/all_to_all | solution.py:628
  61.5 0.7 copy-start.1
  73.7 14.9 %all-to-all-start.2 = ((f32[32,16,128]{2,1,0:T(8,128)}), f32[32,16,128]{2,1,0:T(8,128)S(1)}, u32[]{:S(2)}, u32[]{:S(2)}) async-start(f32[32,16,128]{2,1,0:T(8,128)} %get-tuple-element.32), calls=%async_computation.2 | async-start | bytes 524288 | tf_op jit(solution)/shard_map/all_to_all | solution.py:628
  79.7 95.4 %reduce-scatter.2.cloned.1.call-start = ((), (), s32[]{:S(2)}) async-start(), calls=%async_computation.7 | async-start | bytes 4718592 | tf_op jit(solution)/shard_map/reduce_scatter | solution.py:645
  100.0 16.0 %all-to-all-start.3 = ((f32[32,16,128]{2,1,0:T(8,128)}), f32[32,16,128]{2,1,0:T(8,128)S(1)}, u32[]{:S(2)}, u32[]{:S(2)}) async-start(f32[32,16,128]{2,1,0:T(8,128)} %get-tuple-element.37), calls=%async_computation.3 | async-start | bytes 524288 | tf_op jit(solution)/shard_map/all_to_all | solution.py:628
  130.6 14.1 %all-to-all-start.4 = ((f32[32,24,128]{2,1,0:T(8,128)}), f32[32,24,128]{2,1,0:T(8,128)S(1)}, u32[]{:S(2)}, u32[]{:S(2)}) async-start(f32[32,24,128]{2,1,0:T(8,128)} %get-tuple-element.38), calls=%async_computation.4 | async-start | bytes 786432 | tf_op jit(solution)/shard_map/all_to_all | solution.py:628
  148.3 3.1 %collective-permute-start = (f32[8,128]{1,0:T(8,128)}, f32[8,128]{1,0:T(8,128)S(1)}, u32[]{:S(2)}, u32[]{:S(2)}) collective-permute-start(f32[8,128]{1,0:T(8,128)} %get-tuple-element.43), channel_id=1, source_target_pairs={{0,32},{32,0},{64,96},{96,64},{128,160},{160,128},{192,224},{224,1... | collective-permute-start | bytes 12296 | tf_op jit(solution)/shard_map/ppermute | solution.py:657
  152.1 5.5 %collective-permute-start.1 = (f32[8,128]{1,0:T(8,128)S(1)}, f32[8,128]{1,0:T(8,128)S(1)}, u32[]{:S(2)}, u32[]{:S(2)}) collective-permute-start(f32[8,128]{1,0:T(8,128)S(1)} %add.11), channel_id=1, source_target_pairs={{0,64},{32,96},{64,0},{96,32},{128,192},{160,224},{192,128},{224,1... | collective-permute-start | bytes 12296 | tf_op jit(solution)/shard_map/ppermute | solution.py:657
  152.1 22.3 %all-to-all-start.5 = ((f32[32,32,256]{2,1,0:T(8,128)}), f32[32,32,256]{2,1,0:T(8,128)S(1)}, u32[]{:S(2)}, u32[]{:S(2)}) async-start(f32[32,32,256]{2,1,0:T(8,128)} %get-tuple-element.44), calls=%async_computation.5 | async-start | bytes 2097152 | tf_op jit(solution)/shard_map/all_to_all | solution.py:628
  157.5 14.2 %collective-permute-start.2 = (f32[8,128]{1,0:T(8,128)S(1)}, f32[8,128]{1,0:T(8,128)S(1)}, u32[]{:S(2)}, u32[]{:S(2)}) collective-permute-start(f32[8,128]{1,0:T(8,128)S(1)} %add.12), channel_id=1, source_target_pairs={{0,128},{32,160},{64,192},{96,224},{128,0},{160,32},{192,64},{224,... | collective-permute-start | bytes 12296 | tf_op jit(solution)/shard_map/ppermute | solution.py:657
Sparse Core Ops, SparseCore 0:
  9.8 41.1 all-gather.2
  100.2 52.2 reduce-scatter.1

commit v2 on v1

--- a/solution.py
+++ b/solution.py
@@ -9,6 +9,7 @@
 
 ITERS = 3
 LANES = 128
+STATS_CHUNK = 1024
 S_CHUNK = 512
 T_CHUNK = 1024
 TEACHER_TEMP = 0.07
@@ -83,7 +84,7 @@
     rows, width = sf.shape
     t_rows = tf.shape[0]
     columns = w.shape[1]
-    steps = columns // S_CHUNK
+    steps = columns // STATS_CHUNK
     s_rows, tr = rows // LANES, t_rows // LANES
     lines = -(-(2 * s_rows + tr) // 8) * 8
 
@@ -102,7 +103,7 @@
         before = high[...]
         now = jnp.maximum(before, by_sublane(scores, jnp.max))
         high[...] = now
-        groups = scores.reshape(S_CHUNK // 8, 8, rows)
+        groups = scores.reshape(STATS_CHUNK // 8, 8, rows)
         part = jnp.sum(jnp.exp2((groups - now[None]) * S_SCALE), axis=0)
         total[...] = total[...] * jnp.exp2((before - now) * S_SCALE) + part
         t_high[...] = jnp.maximum(t_high[...], by_sublane(mm(wt, tf_ref[...], NT), jnp.max))
@@ -125,10 +126,10 @@
         [
             whole(sf.shape),
             whole(tf.shape),
-            pl.BlockSpec((width, S_CHUNK), lambda c: (0, c)),
-        ],
-        [
-            pl.BlockSpec((S_CHUNK, width), lambda c: (c, 0)),
+            pl.BlockSpec((width, STATS_CHUNK), lambda c: (0, c)),
+        ],
+        [
+            pl.BlockSpec((STATS_CHUNK, width), lambda c: (c, 0)),
             whole((peers, lines, LANES)),
         ],
         [

time: 186 us -> 187 us (level)
  transfers between devices with their start and end apart: 11 -> 11, of which waited for: 7 -> 7; matrix products, arithmetic and copies ran while one was open for 3% -> 3% of each run, Pallas kernels for 36% -> 35%
where the time goes in v2:
time: 187 us; the launch traced here: 186 us
  Pallas kernels  88.8 us (47%)
  starting transfers between devices  43.9 us (23%)
  waiting for transfers between devices  27.7 us (15%)
  between operations  15.9 us (9%)
  other arithmetic  6.31 us (3%)
  local copies, waits for them, and re-layouts  1.99 us (1%)
    all_to_all x6, starting transfers between devices, swap(): return lax.all_to_all(x, axis, 0, 0)  38.9 us
    all_to_all x6, waiting for transfers between devices, swap(): return lax.all_to_all(x, axis, 0, 0)  24.8 us
    pallas_call x2, Pallas kernels, student_grads(): call(body, steps, in_specs, [whole(ds_shape), pl.BlockSpec((width, S_CHUN...  20.1 us
    pallas_call x1, Pallas kernels, last_iteration(): call(body, steps, [pl.BlockSpec(memory_space=pltpu.SMEM), whole(feats.sha...  13.9 us
    pallas_call x1, Pallas kernels, first_iteration(): call(body, steps, [whole(feats_f32.shape), pl.BlockSpec((blocks, 8, t_row...  11.5 us
    pallas_call x1, Pallas kernels, weight_grad(): call(body, steps, [whole(feats.shape), whole(offset_packed.shape), whole(...  11.1 us
    pallas_call x1, Pallas kernels, next_iteration(): call(body, steps, [whole(feats.shape), whole(old.shape), whole(received.s...  10.7 us
    pallas_call x1, Pallas kernels, student_stats(): call(body, steps, [whole(sf.shape), whole(tf.shape), pl.BlockSpec((width,...  7.75 us
  transfers between devices with their start and end apart: 11, of which 7 were waited for; matrix products, arithmetic and copies ran while one was open for 3% of the time, Pallas kernels for 35%

profile of v2, /device:TPU:1, one launch (start us, length us, event | category | flops | bytes accessed | tf_op | source)
XLA Modules:
  0.0 185.9 jit_solution(13764869757811025918)
XLA Ops:
  7.2 0.0 all-gather.3.cloned.1.call-start
  7.2 1.7 shard_map.67
  8.9 0.0 all-gather.3.cloned.1.call-update
  9.0 0.0 copy-start.2
  9.0 0.0 copy-start.3
  9.0 7.8 %shard_map.68 = (bf16[4096,256]{1,0:T(8,128)(2,1)}, f32[32,24,128]{2,1,0:T(8,128)}) custom-call(bf16[1024,256]{1,0:T(8,128)(2,1)} %sf_ref.5, bf16[256,256]{1,0:T(8,128)(2,1)} %tf_ref.3, bf16[256,4096]{1,0:T(8,128)(2,1)} %w_ref.7), custom_call_target="tpu_custom_call" | custom-call | flops 2684354560 | bytes 8388608 | tf_op jit(solution)/shard_map/pallas_call | solution.py:123
  16.7 8.6 %all-to-all-start = ((f32[32,24,128]{2,1,0:T(8,128)}), f32[32,24,128]{2,1,0:T(8,128)S(1)}, u32[]{:S(2)}, u32[]{:S(2)}) async-start(f32[32,24,128]{2,1,0:T(8,128)} %get-tuple-element.25), calls=%async_computation | async-start | bytes 786432 | tf_op jit(solution)/shard_map/all_to_all | solution.py:629
  25.3 0.0 copy-done.2
  25.4 0.0 copy-done.3
  25.4 1.3 convolution_bitcast_fusion.gt_ref
  26.6 9.0 %all-to-all-done.stats_ref = f32[32,24,128]{2,1,0:T(8,128)S(1)} async-done(((f32[32,24,128]{2,1,0:T(8,128)}), f32[32,24,128]{2,1,0:T(8,128)S(1)}, u32[]{:S(2)}, u32[]{:S(2)}) %all-to-all-start) | async-done | bytes 393248 | tf_op jit(solution)/shard_map/all_to_all | solution.py:629
  35.6 0.7 copy-done
  36.4 1.9 shard_map.69
  38.2 8.2 %all-to-all-start.1 = ((f32[8,40,256]{2,1,0:T(8,128)}), f32[8,40,256]{2,1,0:T(8,128)S(1)}, u32[]{:S(2)}, u32[]{:S(2)}) async-start(f32[8,40,256]{2,1,0:T(8,128)} %get-tuple-element.26), calls=%async_computation.1 | async-start | bytes 655360 | tf_op jit(solution)/shard_map/all_to_all | solution.py:629
  46.4 11.5 %shard_map.70 = (f32[256,1024]{1,0:T(8,128)}, f32[256,4096]{1,0:T(8,128)}) custom-call(bf16[1024,256]{1,0:T(8,128)(2,1)} %sf_ref.5, bf16[256,4096]{1,0:T(8,128)(2,1)} %w_ref.7, bf16[4096,256]{1,0:T(8,128)(2,1)} %get-tuple-element.27.wt_ref, f32[8,128]{1,0:T(8,128)} %get-tuple-element.28.lse_ref), custom_call_target="tpu_custom_call" | custom-call | flops 10737418240 | bytes 6291456 | tf_op jit(solution)/shard_map/pallas_call | solution.py:228
  57.9 3.0 %all-to-all-done.1.shared_ref.sh_ref = f32[8,40,256]{2,1,0:T(8,128)S(1)} async-done(((f32[8,40,256]{2,1,0:T(8,128)}), f32[8,40,256]{2,1,0:T(8,128)S(1)}, u32[]{:S(2)}, u32[]{:S(2)}) %all-to-all-start.1) | async-done | bytes 327712 | tf_op jit(solution)/shard_map/all_to_all | solution.py:629
  60.9 0.7 copy-done.1
  61.6 11.5 %shard_map.71 = (bf16[8,256,256]{2,1,0:T(8,128)(2,1)}, f32[16,128]{1,0:T(8,128)}, f32[32,16,128]{2,1,0:T(8,128)}, f32[256,4096]{1,0:T(8,128)}) custom-call(f32[8,256,256]{2,1,0:T(8,128)} %bitcast.7, f32[8,40,256]{2,1,0:T(8,128)} %copy-done.1, bf16[4096,256]{1,0:T(8,128)(2,1)} %get-tuple-element.27.wt_ref, ...), custom_call_target="tpu_custom_call", output_to_operand_aliasing={{3}: (3, {})} | custom-call | flops 10737418240 | bytes 5242880 | tf_op jit(solution)/shard_map/pallas_call | solution.py:306
  73.2 6.1 %all-to-all-start.2 = ((f32[32,16,128]{2,1,0:T(8,128)}), f32[32,16,128]{2,1,0:T(8,128)S(1)}, u32[]{:S(2)}, u32[]{:S(2)}) async-start(f32[32,16,128]{2,1,0:T(8,128)} %get-tuple-element.32), calls=%async_computation.2 | async-start | bytes 524288 | tf_op jit(solution)/shard_map/all_to_all | solution.py:629
  79.2 0.0 reduce-scatter.2.cloned.1.call-start
  79.3 8.6 %shard_map.72 = (f32[32,32,256]{2,1,0:T(8,128)}, f32[256,4096]{1,0:T(8,128)}) custom-call(bf16[1024,256]{1,0:T(8,128)(2,1)} %sf_ref.5, bf16[256,4096]{1,0:T(8,128)(2,1)} %w_ref.7, bf16[4096,256]{1,0:T(8,128)(2,1)} %get-tuple-element.27.wt_ref, f32[8,128]{1,0:T(8,128)} %get-tuple-element.28.lse_ref, ...), custom_call_target="tpu_custom_call", output_to_operand_aliasing={{1}: (4, {})} | custom-call | flops 6442450944 | bytes 6291456 | tf_op jit(solution)/shard_map/pallas_call | solution.py:228
  87.9 0.4 all-to-all-done.2
  88.2 0.6 reduce_sum.36.recv_ref
  88.9 10.7 %shard_map.73 = (f32[16,128]{1,0:T(8,128)}, f32[32,16,128]{2,1,0:T(8,128)}, f32[256,4096]{1,0:T(8,128)}) custom-call(bf16[8,256,256]{2,1,0:T(8,128)(2,1)} %get-tuple-element.30.feat_ref, f32[16,128]{1,0:T(8,128)} %get-tuple-element.31.old_ref, f32[16,128]{1,0:T(8,128)} %reduce_sum.36.recv_ref, ...), custom_call_target="tpu_custom_call", output_to_operand_aliasing={{2}: (4, {})} | custom-call | flops 10737418240 | bytes 4194304 | tf_op jit(solution)/shard_map/pallas_call | solution.py:368
  99.6 0.0 reduce-scatter.2.cloned.1.call-update
  99.6 7.0 %all-to-all-start.3 = ((f32[32,16,128]{2,1,0:T(8,128)}), f32[32,16,128]{2,1,0:T(8,128)S(1)}, u32[]{:S(2)}, u32[]{:S(2)}) async-start(f32[32,16,128]{2,1,0:T(8,128)} %get-tuple-element.37), calls=%async_computation.3 | async-start | bytes 524288 | tf_op jit(solution)/shard_map/all_to_all | solution.py:629
  106.6 1.0 fusion.oh_ref
  107.6 8.0 %all-to-all-done.3 = f32[32,16,128]{2,1,0:T(8,128)S(1)} async-done(((f32[32,16,128]{2,1,0:T(8,128)}), f32[32,16,128]{2,1,0:T(8,128)S(1)}, u32[]{:S(2)}, u32[]{:S(2)}) %all-to-all-start.3) | async-done | bytes 262176 | tf_op jit(solution)/shard_map/all_to_all | solution.py:629
  115.6 0.6 reduce_sum.37.recv_ref
  116.2 13.9 %shard_map.74 = (f32[16,128]{1,0:T(8,128)}, f32[4096,128]{1,0:T(8,128)}, f32[256,256]{1,0:T(8,128)}, f32[32,24,128]{2,1,0:T(8,128)}) custom-call(s32[1]{0:T(128)} %bitcast.me_ref, bf16[8,256,256]{2,1,0:T(8,128)(2,1)} %get-tuple-element.30.feat_ref, f32[16,128]{1,0:T(8,128)} %get-tuple-element.36.old_ref, f32[16,128]{1,0:T(8,128)} %reduce_sum.37.recv_ref, ...), custom_call_target="tpu_custom_call" | custom-call | flops 5368709120 | bytes 8388608 | tf_op jit(solution)/shard_map/pallas_call | solution.py:441
  130.1 3.7 %all-to-all-start.4 = ((f32[32,24,128]{2,1,0:T(8,128)}), f32[32,24,128]{2,1,0:T(8,128)S(1)}, u32[]{:S(2)}, u32[]{:S(2)}) async-start(f32[32,24,128]{2,1,0:T(8,128)} %get-tuple-element.38), calls=%async_computation.4 | async-start | bytes 786432 | tf_op jit(solution)/shard_map/all_to_all | solution.py:629
  133.8 7.2 %shard_map.75._.near_ref = bf16[8,2048,256]{2,1,0:T(8,128)(2,1)} custom-call(bf16[8,256,256]{2,1,0:T(8,128)(2,1)} %get-tuple-element.30.feat_ref, f32[16,128]{1,0:T(8,128)} %get-tuple-element.41.off_ref, bf16[4096,256]{1,0:T(8,128)(2,1)} %get-tuple-element.27.wt_ref, f32[4096,128]{1,0:T(8,128)} %get-tuple-element.42.scale_ref), custom_call_target="tpu_custom_call" | custom-call | flops 4294967296 | bytes 10485760 | tf_op jit(solution)/shard_map/pallas_call | solution.py:542
  141.1 3.2 %all-to-all-done.4 = f32[32,24,128]{2,1,0:T(8,128)S(1)} async-done(((f32[32,24,128]{2,1,0:T(8,128)}), f32[32,24,128]{2,1,0:T(8,128)S(1)}, u32[]{:S(2)}, u32[]{:S(2)}) %all-to-all-start.4) | async-done | bytes 393248 | tf_op jit(solution)/shard_map/all_to_all | solution.py:629
  144.3 0.6 reduce_sum.38.recv_ref
  144.9 3.0 %shard_map.76 = (f32[8,128]{1,0:T(8,128)}, f32[16,128]{1,0:T(8,128)}, f32[32,32,256]{2,1,0:T(8,128)}) custom-call(s32[1]{0:T(128)} %bitcast.me_ref, f32[24,128]{1,0:T(8,128)} %reduce_sum.38.recv_ref, f32[8,128]{1,0:T(8,128)} %get-tuple-element.28.lse_ref, f32[256,256]{1,0:T(8,128)} %get-tuple-element.39.taught_ref, bf16[1024,256]{1,0:T(8,128)(2,1)} %fusion.oh_ref, ...), custom_call_target="tpu_custom_call" | custom-call | flops 268435456 | bytes 3145728 | tf_op jit(solution)/shard_map/pallas_call | solution.py:498
  147.9 0.4 collective-permute-start
  148.3 2.9 %collective-permute-done = f32[8,128]{1,0:T(8,128)S(1)} collective-permute-done((f32[8,128]{1,0:T(8,128)}, f32[8,128]{1,0:T(8,128)S(1)}, u32[]{:S(2)}, u32[]{:S(2)}) %collective-permute-start) | collective-permute-done | bytes 4128 | tf_op jit(solution)/shard_map/ppermute | solution.py:658
  151.2 0.7 add.11
  151.9 1.1 collective-permute-start.1
  153.0 5.3 %all-to-all-start.5 = ((f32[32,32,256]{2,1,0:T(8,128)}), f32[32,32,256]{2,1,0:T(8,128)S(1)}, u32[]{:S(2)}, u32[]{:S(2)}) async-start(f32[32,32,256]{2,1,0:T(8,128)} %get-tuple-element.44), calls=%async_computation.5 | async-start | bytes 2097152 | tf_op jit(solution)/shard_map/all_to_all | solution.py:629
  158.3 0.0 collective-permute-done.1
  158.3 3.4 %collective-permute-start.2 = (f32[8,128]{1,0:T(8,128)S(1)}, f32[8,128]{1,0:T(8,128)S(1)}, u32[]{:S(2)}, u32[]{:S(2)}) collective-permute-start(f32[8,128]{1,0:T(8,128)S(1)} %add.12), channel_id=1, source_target_pairs={{0,128},{32,160},{64,192},{96,224},{128,0},{160,32},{192,64},{224,... | collective-permute-start | bytes 12296 | tf_op jit(solution)/shard_map/ppermute | solution.py:658
  161.7 11.1 %shard_map.77 = f32[32,4096]{1,0:T(8,128)} custom-call(bf16[8,256,256]{2,1,0:T(8,128)(2,1)} %get-tuple-element.30.feat_ref, f32[16,128]{1,0:T(8,128)} %get-tuple-element.41.off_ref, f32[16,128]{1,0:T(8,128)} %get-tuple-element.46.inv_ref, bf16[4096,256]{1,0:T(8,128)(2,1)} %get-tuple-element.27.wt_ref, f32[8,40,256]{2,1,0:T(8,128)} %copy-done.1, ...), custom_call_target="tpu_custom_call" | custom-call | flops 12884901888 | bytes 14680064 | tf_op jit(solution)/shard_map/pallas_call | solution.py:595
  172.8 0.0 collective-permute-done.2
  172.8 0.5 slice.3
  174.0 1.3 all-to-all-done.5
  175.2 0.7 reduce_sum.39
  175.9 2.0 %sub.16 = f32[32,4096]{1,0:T(8,128)} subtract(f32[32,4096]{1,0:T(8,128)} %reduce-scatter.2.cloned.1.call-done, f32[32,4096]{1,0:T(8,128)} %shard_map.77) | non-fusion elementwise | flops 131072 | bytes 1572864 | tf_op jit(solution)/shard_map/sub | solution.py:660
  (7 shorter events, 0.0 us)
Async XLA Ops:
  7.2 53.8 %all-gather.3.cloned.1.call-start = ((), (), s32[]{:S(2)}) async-start(), calls=%async_computation.8 | async-start | bytes 2359296 | tf_op jit(solution)/shard_map/all_gather | solution.py:631
  9.0 16.4 %copy-start.2 = (s32[1024]{0:T(1024)S(1)}, s32[1024]{0:T(1024)}, u32[]{:S(2)}) copy-start(s32[1024]{0:T(1024)} %param.7) | copy-start | bytes 12292
  9.0 16.4 %copy-start.3 = (bf16[1024,256]{1,0:T(8,128)(2,1)S(1)}, bf16[1024,256]{1,0:T(8,128)(2,1)}, u32[]{:S(2)}) copy-start(bf16[1024,256]{1,0:T(8,128)(2,1)} %sf_ref.5) | copy-start | bytes 1572868
  16.7 18.9 %all-to-all-start = ((f32[32,24,128]{2,1,0:T(8,128)}), f32[32,24,128]{2,1,0:T(8,128)S(1)}, u32[]{:S(2)}, u32[]{:S(2)}) async-start(f32[32,24,128]{2,1,0:T(8,128)} %get-tuple-element.25), calls=%async_computation | async-start | bytes 786432 | tf_op jit(solution)/shard_map/all_to_all | solution.py:629
  35.6 0.7 copy-start
  38.2 22.7 %all-to-all-start.1 = ((f32[8,40,256]{2,1,0:T(8,128)}), f32[8,40,256]{2,1,0:T(8,128)S(1)}, u32[]{:S(2)}, u32[]{:S(2)}) async-start(f32[8,40,256]{2,1,0:T(8,128)} %get-tuple-element.26), calls=%async_computation.1 | async-start | bytes 655360 | tf_op jit(solution)/shard_map/all_to_all | solution.py:629
  60.9 0.7 copy-start.1
  73.2 15.1 %all-to-all-start.2 = ((f32[32,16,128]{2,1,0:T(8,128)}), f32[32,16,128]{2,1,0:T(8,128)S(1)}, u32[]{:S(2)}, u32[]{:S(2)}) async-start(f32[32,16,128]{2,1,0:T(8,128)} %get-tuple-element.32), calls=%async_computation.2 | async-start | bytes 524288 | tf_op jit(solution)/shard_map/all_to_all | solution.py:629
  79.2 96.7 %reduce-scatter.2.cloned.1.call-start = ((), (), s32[]{:S(2)}) async-start(), calls=%async_computation.7 | async-start | bytes 4718592 | tf_op jit(solution)/shard_map/reduce_scatter | solution.py:646
  99.6 16.0 %all-to-all-start.3 = ((f32[32,16,128]{2,1,0:T(8,128)}), f32[32,16,128]{2,1,0:T(8,128)S(1)}, u32[]{:S(2)}, u32[]{:S(2)}) async-start(f32[32,16,128]{2,1,0:T(8,128)} %get-tuple-element.37), calls=%async_computation.3 | async-start | bytes 524288 | tf_op jit(solution)/shard_map/all_to_all | solution.py:629
  130.1 14.2 %all-to-all-start.4 = ((f32[32,24,128]{2,1,0:T(8,128)}), f32[32,24,128]{2,1,0:T(8,128)S(1)}, u32[]{:S(2)}, u32[]{:S(2)}) async-start(f32[32,24,128]{2,1,0:T(8,128)} %get-tuple-element.38), calls=%async_computation.4 | async-start | bytes 786432 | tf_op jit(solution)/shard_map/all_to_all | solution.py:629
  147.9 3.3 %collective-permute-start = (f32[8,128]{1,0:T(8,128)}, f32[8,128]{1,0:T(8,128)S(1)}, u32[]{:S(2)}, u32[]{:S(2)}) collective-permute-start(f32[8,128]{1,0:T(8,128)} %get-tuple-element.43), channel_id=1, source_target_pairs={{0,32},{32,0},{64,96},{96,64},{128,160},{160,128},{192,224},{224,1... | collective-permute-start | bytes 12296 | tf_op jit(solution)/shard_map/ppermute | solution.py:658
  151.9 6.5 %collective-permute-start.1 = (f32[8,128]{1,0:T(8,128)S(1)}, f32[8,128]{1,0:T(8,128)S(1)}, u32[]{:S(2)}, u32[]{:S(2)}) collective-permute-start(f32[8,128]{1,0:T(8,128)S(1)} %add.11), channel_id=1, source_target_pairs={{0,64},{32,96},{64,0},{96,32},{128,192},{160,224},{192,128},{224,1... | collective-permute-start | bytes 12296 | tf_op jit(solution)/shard_map/ppermute | solution.py:658
  153.0 22.3 %all-to-all-start.5 = ((f32[32,32,256]{2,1,0:T(8,128)}), f32[32,32,256]{2,1,0:T(8,128)S(1)}, u32[]{:S(2)}, u32[]{:S(2)}) async-start(f32[32,32,256]{2,1,0:T(8,128)} %get-tuple-element.44), calls=%async_computation.5 | async-start | bytes 2097152 | tf_op jit(solution)/shard_map/all_to_all | solution.py:629
  158.3 14.5 %collective-permute-start.2 = (f32[8,128]{1,0:T(8,128)S(1)}, f32[8,128]{1,0:T(8,128)S(1)}, u32[]{:S(2)}, u32[]{:S(2)}) collective-permute-start(f32[8,128]{1,0:T(8,128)S(1)} %add.12), channel_id=1, source_target_pairs={{0,128},{32,160},{64,192},{96,224},{128,0},{160,32},{192,64},{224,... | collective-permute-start | bytes 12296 | tf_op jit(solution)/shard_map/ppermute | solution.py:658
Sparse Core Ops, SparseCore 0:
  9.8 42.5 all-gather.2
  99.7 54.0 reduce-scatter.1
